TPU v7x, 512 devices: a whole 4x8x8 slice. The times are simulated.
512 devices in a mesh: seq: 32 (over x, y), batch: 16 (over z, core).
Axes of the slice: x: 4, y: 8, z: 8, core: 2. Of those that a mesh axis runs over, the one named last changes fastest.
Arguments:
- query: bfloat16 [32, 4, 64, 576], P('batch', None, 'seq'), may hold values from -48 to 48
- cache: bfloat16 [32, 65536, 576], P('batch', 'seq'), may hold values from -6 to 6
- lengths: int32 [32], P('batch'), may hold values from 4 to 65536
- value_up: bfloat16 [64, 512, 128], P('batch'), may hold values from -0.25 to 0.25
- out_weight: bfloat16 [8192, 7168], P('batch', 'seq'), may hold values from -0.0625 to 0.0625
Outputs:
- mixed: bfloat16 [32, 4, 7168], P('batch', None, 'seq')
All inputs are finite; a program needn't handle non-finite values.
Results may differ from a plain program's by a relative error of at most 0.0075.
Values may be sent and summed in bfloat16 or wider, within the bound.
No kernel may reach another device: no remote copies, remote signals or barrier semaphores. Data moves between devices by JAX's collectives and lax.ppermute only.
A program may use at most 128 MiB of HBM per device.

v0:
```python
import jax
import jax.numpy as jnp
from jax import lax
from jax.sharding import PartitionSpec as P

ROPE = 64
NOPE = 128


NEG = -1e30


def per_device(query, cache, lengths, value_up, out_weight):
    queries = lax.all_gather(query, "seq", axis=2, tiled=True)
    ahead = queries.shape[1]
    ctx_dev = cache.shape[1]
    latent = value_up.shape[1]
    scale = 1.0 / (NOPE + ROPE) ** 0.5
    scores = (
        jnp.einsum("bthk,bpk->bthp", queries, cache, preferred_element_type=jnp.float32) * scale
    )
    position = lax.axis_index("seq") * ctx_dev + jnp.arange(ctx_dev, dtype=jnp.int32)
    limit = lengths[:, None] - ahead + 1 + jnp.arange(ahead, dtype=jnp.int32)[None, :]
    allowed = position[None, None, None, :] < limit[:, :, None, None]
    masked = jnp.where(allowed, scores, NEG)
    block_top = jnp.max(masked, axis=3)
    weights = jnp.where(allowed, jnp.exp(masked - block_top[..., None]), 0.0)
    block_total = jnp.sum(weights, axis=3)
    block_out = jnp.einsum(
        "bthp,bpl->bthl",
        weights.astype(jnp.bfloat16),
        cache[:, :, :latent],
        preferred_element_type=jnp.float32,
    )
    top = lax.pmax(block_top, "seq")
    factor = jnp.exp(block_top - top)
    total, summed = lax.psum((block_total * factor, block_out * factor[..., None]), "seq")
    attended = (summed / total[..., None]).astype(jnp.bfloat16)
    values = jnp.einsum(
        "bnhl,hlv->bnhv",
        lax.all_to_all(attended, "batch", split_axis=2, concat_axis=0, tiled=True),
        value_up,
        preferred_element_type=jnp.float32,
    ).astype(jnp.bfloat16)
    flat = values.reshape(values.shape[0], values.shape[1], values.shape[2] * values.shape[3])
    terms = jnp.einsum("bnk,kd->bnd", flat, out_weight, preferred_element_type=jnp.float32)
    return lax.psum_scatter(terms, "batch", scatter_dimension=0, tiled=True).astype(jnp.bfloat16)


def solution(mesh):
    placed = (
        P("batch", None, "seq", None),
        P("batch", "seq", None),
        P("batch"),
        P("batch", None, None),
        P("batch", "seq"),
    )
    return jax.shard_map(
        per_device, mesh=mesh, in_specs=placed, out_specs=P("batch", None, "seq"), check_vma=False
    )
```

profile of v0, /device:TPU:1, one launch (start us, length us, event | category | flops | bytes accessed | tf_op | source)
XLA Modules:
  0.0 383.9 jit_solution(1849897164065453909)
XLA Ops:
  6.5 0.0 copy-start
  6.5 0.0 all-reduce.3.cloned.1.call-start
  6.5 0.7 broadcast_add_fusion
  7.3 0.1 iota_add_fusion.1
  7.3 0.7 copy.13
  8.1 39.9 %all_gather.3 = bf16[2,4,64,576]{3,1,0,2:T(4,128)(2,1)S(1)} all-gather(bf16[2,4,2,576]{3,1,0,2:T(4,128)(2,1)S(1)} %copy.13), channel_id=1, replica_groups=mesh['seq'=32,'batch'=16] {'seq'}, dimensions={2}, use_global_device_ids=true | all-gather | bytes 608256 | tf_op jit(solution)/shard_map/all_gather | solution.py:14
  48.0 0.1 broadcast_compare_fusion
  48.1 6.2 %fusion.5 = (f32[2,4,64]{2,1,0:T(4,128)S(1)}, f32[2,4,64,2048]{3,2,1,0:T(8,128)}) fusion(pred[2,4,2048]{2,1,0:T(4,128)(4,1)S(1)} %broadcast_compare_fusion, bf16[2,2048,576]{1,2,0:T(8,128)(2,1)} %param.6, bf16[2,4,64,576]{3,1,0,2:T(4,128)(2,1)S(1)} %all_gather.3), kind=kOutput, calls=%fused_computation.7 | convolution fusion | flops 1211104768 | bytes 9521152 | tf_op jit(solution)/shard_map/bthk,bpk->bthp/dot_general | solution.py:20
  54.2 58.1 %pmax.7 = f32[2,4,64]{2,1,0:T(4,128)S(1)} all-reduce(f32[2,4,64]{2,1,0:T(4,128)S(1)} %get-tuple-element.7), channel_id=1, replica_groups=mesh['seq'=32,'batch'=16] {'seq'}, use_global_device_ids=true, to_apply=%region_1.2 | all-reduce | flops 512 | bytes 4096 | tf_op jit(solution)/shard_map/pmax | solution.py:35
  112.3 0.0 copy-start.1
  112.3 3.6 fusion.6
  116.0 0.0 copy-done.1
  116.0 4.7 %fusion.14 = f32[2,4,64,512]{3,2,1,0:T(8,128)} fusion(bf16[2,2048,576]{1,2,0:T(8,128)(2,1)} %param.6, f32[2,4,64,2048]{3,2,1,0:T(8,128)S(1)} %copy-done.1, f32[2,4,64]{2,1,0:T(4,128)S(1)} %get-tuple-element.7, pred[2,4,2048]{2,1,0:T(4,128)(4,1)S(1)} %broadcast_compare_fusion, f32[2,4,64]{2,1,0:T(4,128)S(1)} %bitcast.48), kind=kOutput, calls=%fused_computation.15 | convolution fusion | flops 1079246848 | bytes 9457664 | tf_op jit(solution)/shard_map/bthp,bpl->bthl/dot_general | solution.py:29
  120.7 0.0 copy-start.2
  120.7 0.0 all-reduce.3.cloned.1.call-update
  120.7 56.1 %psum.15 = f32[2,4,64]{2,1,0:T(4,128)S(1)} all-reduce(f32[2,4,64]{2,1,0:T(4,128)S(1)} %bitcast.45), channel_id=1, replica_groups=mesh['seq'=32,'batch'=16] {'seq'}, use_global_device_ids=true, to_apply=%region_4.5 | all-reduce | flops 512 | bytes 4096 | tf_op jit(solution)/shard_map/psum | solution.py:37
  176.8 122.5 %all-reduce.3.cloned.1.call-done = f32[2,4,64,512]{3,2,1,0:T(8,128)} async-done(((f32[2,4,64,512]{3,2,1,0:T(8,128)}), f32[2,4,64,512]{3,2,1,0:T(8,128)}) %all-reduce.3.cloned.1.call-update) | async-done | bytes 1048592 | tf_op jit(solution)/shard_map/psum | solution.py:37
  299.3 1.4 divide_convert_fusion
  300.7 1.2 copy.16
  301.9 12.6 %all-to-all-start = ((bf16[2,4,64,512]{3,1,0,2:T(4,128)(2,1)}), bf16[2,4,64,512]{3,1,0,2:T(4,128)(2,1)S(1)}, u32[]{:S(2)}, u32[]{:S(2)}) async-start(bf16[2,4,64,512]{3,1,0,2:T(4,128)(2,1)} %copy.16), calls=%async_computation | async-start | bytes 1048576 | tf_op jit(solution)/shard_map/all_to_all | solution.py:41
  314.5 1.3 dynamic-slice
  316.4 15.4 %all-to-all-done = bf16[2,4,64,512]{3,1,0,2:T(4,128)(2,1)S(1)} async-done(((bf16[2,4,64,512]{3,1,0,2:T(4,128)(2,1)}), bf16[2,4,64,512]{3,1,0,2:T(4,128)(2,1)S(1)}, u32[]{:S(2)}, u32[]{:S(2)}) %all-to-all-start) | async-done | bytes 524320 | tf_op jit(solution)/shard_map/all_to_all | solution.py:41
  331.8 0.4 copy.34
  332.2 0.2 all_to_all.16
  332.4 0.0 copy-done
  332.4 0.3 fusion.19
  332.7 0.0 copy-done.2
  332.7 0.2 fusion.22
  333.0 0.1 copy.19
  333.1 43.4 %all-reduce = bf16[32,4,224]{2,1,0:T(4,128)(2,1)S(1)} all-reduce(f32[32,4,224]{2,1,0:T(4,128)S(1)} %copy.19), channel_id=2, replica_groups=mesh['seq'=32,'batch'=16] {'batch'}, use_global_device_ids=true, to_apply=%region_5.6.clone | all-reduce | flops 28672 | bytes 172032
  376.5 0.6 dynamic-slice_convert_fusion
  (2 shorter events, 0.0 us)
Async XLA Ops:
  6.5 325.9 %copy-start = (bf16[4,512,128]{2,1,0:T(8,128)(2,1)S(1)}, bf16[4,512,128]{2,1,0:T(8,128)(2,1)}, u32[]{:S(2)}) copy-start(bf16[4,512,128]{2,1,0:T(8,128)(2,1)} %param.8) | copy-start | bytes 1572868
  6.5 292.8 %all-reduce.3.cloned.1.call-start = ((), (), s32[]{:S(2)}) async-start(), calls=%async_computation.1 | async-start | bytes 2097152 | tf_op jit(solution)/shard_map/psum | solution.py:37
  112.3 3.7 copy-start.1
  120.7 212.1 %copy-start.2 = (bf16[512,224]{0,1:T(8,128)(2,1)S(1)}, bf16[512,224]{0,1:T(8,128)(2,1)}, u32[]{:S(2)}) copy-start(bf16[512,224]{0,1:T(8,128)(2,1)} %param.9) | copy-start | bytes 688132
  301.9 29.9 %all-to-all-start = ((bf16[2,4,64,512]{3,1,0,2:T(4,128)(2,1)}), bf16[2,4,64,512]{3,1,0,2:T(4,128)(2,1)S(1)}, u32[]{:S(2)}, u32[]{:S(2)}) async-start(bf16[2,4,64,512]{3,1,0,2:T(4,128)(2,1)} %copy.16), calls=%async_computation | async-start | bytes 1048576 | tf_op jit(solution)/shard_map/all_to_all | solution.py:41
Sparse Core Ops, SparseCore 0:
  120.8 178.4 all-reduce.2
where the time goes:
time: 385 us; the launch traced here: 384 us
  blocking collectives  198 us (51%)
  waiting for transfers between devices  138 us (36%)
  between operations  14.1 us (4%)
  starting transfers between devices  12.6 us (3%)
  matrix products  11.3 us (3%)
  other arithmetic  5.9 us (2%)
  local copies, waits for them, and re-layouts  4.53 us (1%)
    psum x1, waiting for transfers between devices, per_device(): lax.psum((block_total * factor, block_out * factor[..., None]), 'seq')  122 us
    pmax x1, blocking collectives, per_device(): top = lax.pmax(block_top, 'seq')  58.1 us
    psum x1, blocking collectives, per_device(): lax.psum((block_total * factor, block_out * factor[..., None]), 'seq')  56.1 us
    unnamed x1, blocking collectives  43.4 us
    all_gather x1, blocking collectives, per_device(): queries = lax.all_gather(query, 'seq', axis=2, tiled=True)  39.9 us
    all_to_all x1, waiting for transfers between devices, per_device(): lax.all_to_all(attended, 'batch', split_axis=2, concat_axis=0, tiled=True)  15.4 us
    all_to_all x1, starting transfers between devices, per_device(): lax.all_to_all(attended, 'batch', split_axis=2, concat_axis=0, tiled=True)  12.6 us
  transfers between devices with their start and end apart: 2, of which 2 were waited for; matrix products, arithmetic and copies ran while one was open for 0% of the time, Pallas kernels for 0%

commit v1 on v0

v1 whole, which is shorter than its diff:
```python
import jax
import jax.numpy as jnp
from jax import lax
from jax.sharding import PartitionSpec as P

ROPE = 64
NOPE = 128


NEG = -1e30


def per_device(query, cache, lengths, value_up, out_weight):
    n_seq = lax.axis_size("seq")
    n_batch = lax.axis_size("batch")
    seqs, ahead, own, width = query.shape
    ctx_dev = cache.shape[1]
    held, latent, vdim = value_up.shape
    scale = 1.0 / (NOPE + ROPE) ** 0.5
    seq = lax.axis_index("seq")

    rows = lax.all_gather(out_weight, "batch", axis=0, tiled=True)
    per_group = held // own
    part = lax.rem(seq, per_group) * own
    mine = lax.dynamic_slice_in_dim(value_up, part, own, 0)
    pairs = []
    for s in range(n_seq):
        for g in range(n_batch):
            source = (per_group * g + s % per_group) * n_batch + s // per_group
            pairs.append((source, s * n_batch + g))
    up = lax.ppermute(mine, ("seq", "batch"), pairs)

    sent = query.reshape(1, seqs, ahead * own, width)
    queries = lax.all_to_all(
        jnp.broadcast_to(sent, (n_seq,) + sent.shape[1:]), "seq", 0, 0, tiled=True
    )
    scores = (
        jnp.einsum("sbrk,bpk->bsrp", queries, cache, preferred_element_type=jnp.float32) * scale
    )
    position = seq * ctx_dev + jnp.arange(ctx_dev, dtype=jnp.int32)
    limit = lengths[:, None] - ahead + 1 + jnp.arange(ahead * own, dtype=jnp.int32)[None, :] // own
    allowed = position[None, None, None, :] < limit[:, None, :, None]
    masked = jnp.where(allowed, scores, NEG)
    block_top = jnp.max(masked, axis=3).astype(jnp.bfloat16)
    weights = jnp.where(allowed, jnp.exp(masked - block_top.astype(jnp.float32)[..., None]), 0.0)
    block_total = jnp.sum(weights, axis=3)
    block_out = jnp.einsum(
        "bsrp,bpl->bsrl",
        weights.astype(jnp.bfloat16),
        cache[:, :, :latent],
        preferred_element_type=jnp.float32,
    )
    high = block_total.astype(jnp.bfloat16)
    low = (block_total - high.astype(jnp.float32)).astype(jnp.bfloat16)
    extra = jnp.stack([block_top, high, low], axis=-1)
    extra = jnp.pad(extra, ((0, 0), (0, 0), (0, 0), (0, 125)))
    parts = jnp.concatenate([block_out.astype(jnp.bfloat16), extra], axis=-1)
    parts = lax.all_to_all(parts.transpose(1, 0, 2, 3), "seq", 0, 0, tiled=True).astype(jnp.float32)
    block_top, block_total = parts[..., latent], parts[..., latent + 1] + parts[..., latent + 2]
    factor = jnp.exp(block_top - jnp.max(block_top, axis=0))
    total = jnp.sum(block_total * factor, axis=0)
    attended = jnp.sum(parts[..., :latent] * factor[..., None], axis=0) / total[..., None]
    attended = attended.astype(jnp.bfloat16).reshape(seqs, ahead, own, latent)
    values = jnp.einsum(
        "bthl,hlv->bthv", attended, up, preferred_element_type=jnp.float32
    ).astype(jnp.bfloat16)
    values = lax.all_to_all(
        jnp.broadcast_to(values[None], (n_seq,) + values.shape), "seq", 0, 0, tiled=True
    )
    flat = values.transpose(1, 2, 0, 3, 4).reshape(seqs, ahead, n_seq * own * vdim)
    return jnp.einsum("btk,kd->btd", flat, rows, preferred_element_type=jnp.float32).astype(
        jnp.bfloat16
    )


def solution(mesh):
    placed = (
        P("batch", None, "seq", None),
        P("batch", "seq", None),
        P("batch"),
        P("batch", None, None),
        P("batch", "seq"),
    )
    return jax.shard_map(
        per_device, mesh=mesh, in_specs=placed, out_specs=P("batch", None, "seq"), check_vma=False
    )
```

time: 385 us -> 130 us (0.34)
  blocking collectives: 198 us -> 34.3 us
  waiting for transfers between devices: 138 us -> 27.3 us
  starting transfers between devices: 12.6 us -> 24.6 us
  matrix products: 11.3 us -> 15.9 us
    psum x1 -> x0, waiting for transfers between devices: 122 us -> none  [per_device(): lax.psum((block_total * factor, block_out * factor[..., None]), 'seq')]
    pmax x1 -> x0, blocking collectives: 58.1 us -> none  [per_device(): top = lax.pmax(block_top, 'seq')]
    psum x1 -> x0, blocking collectives: 56.1 us -> none  [per_device(): lax.psum((block_total * factor, block_out * factor[..., None]), 'seq')]
    unnamed x1 -> x0, blocking collectives: 43.4 us -> none
    all_gather x1 -> x0, blocking collectives: 39.9 us -> none  [per_device(): queries = lax.all_gather(query, 'seq', axis=2, tiled=True)]
    all_to_all x0 -> x1, blocking collectives: none -> 34.3 us  [per_device(): lax.all_to_all(jnp.broadcast_to(values[None], (n_seq,) + values.shape), '...]
    all_to_all x1 -> x2, waiting for transfers between devices: 15.4 us -> 26.6 us  [the longest x1 15.5 us: per_device(): lax.all_to_all(jnp.broadcast_to(sent, (n_seq,) + sent.shape[1:]), 'seq',...]
    all_to_all x1 -> x2, starting transfers between devices: 12.6 us -> 19 us  [the longest x1 10.5 us: per_device(): lax.all_to_all(jnp.broadcast_to(sent, (n_seq,) + sent.shape[1:]), 'seq',...]
  transfers between devices with their start and end apart: 2 -> 4, of which waited for: 2 -> 2; matrix products, arithmetic and copies ran while one was open for 0% -> 20% of each run, Pallas kernels for 0% -> 0%
where the time goes in v1:
time: 130 us; the launch traced here: 129 us
  blocking collectives  34.3 us (26%)
  waiting for transfers between devices  27.3 us (21%)
  starting transfers between devices  24.6 us (19%)
  matrix products  15.9 us (12%)
  between operations  13.6 us (10%)
  local copies, waits for them, and re-layouts  7.5 us (6%)
  other arithmetic  6.15 us (5%)
    all_to_all x1, blocking collectives, per_device(): lax.all_to_all(jnp.broadcast_to(values[None], (n_seq,) + values.shape), '...  34.3 us
    all_to_all x1, waiting for transfers between devices, per_device(): lax.all_to_all(jnp.broadcast_to(sent, (n_seq,) + sent.shape[1:]), 'seq',...  15.5 us
    all_to_all x1, waiting for transfers between devices, per_device(): lax.all_to_all(parts.transpose(1, 0, 2, 3), 'seq', 0, 0, tiled=True)  11.1 us
    all_to_all x1, starting transfers between devices, per_device(): lax.all_to_all(jnp.broadcast_to(sent, (n_seq,) + sent.shape[1:]), 'seq',...  10.5 us
    all_to_all x1, starting transfers between devices, per_device(): lax.all_to_all(parts.transpose(1, 0, 2, 3), 'seq', 0, 0, tiled=True)  8.53 us
    dot_general x1, matrix products, per_device(): jnp.einsum('sbrk,bpk->bsrp', queries, cache, preferred_element_type=jnp.f...  6.22 us
    ppermute x1, starting transfers between devices, per_device(): up = lax.ppermute(mine, ('seq', 'batch'), pairs)  5.58 us
    dot_general x1, matrix products, per_device(): jnp.einsum('bsrp,bpl->bsrl', weights.astype(jnp.bfloat16), cache[:, :, :l...  4.88 us
  transfers between devices with their start and end apart: 4, of which 2 were waited for; matrix products, arithmetic and copies ran while one was open for 20% of the time, Pallas kernels for 0%

profile of v1, /device:TPU:1, one launch (start us, length us, event | category | flops | bytes accessed | tf_op | source)
XLA Modules:
  0.0 129.4 jit_solution(17649322370405995623)
XLA Ops:
  6.5 0.0 copy-start
  6.5 0.0 all-gather.2.cloned.1.call-start
  6.5 0.7 all-gather.2.cloned.1.call-update
  7.3 0.8 broadcast_in_dim.40
  8.0 0.9 broadcast_in_dim.41
  8.9 10.5 %all-to-all-start = ((bf16[32,2,8,576]{3,2,1,0:T(8,128)(2,1)}), bf16[32,2,8,576]{3,2,1,0:T(8,128)(2,1)S(1)}, u32[]{:S(2)}, u32[]{:S(2)}) async-start(bf16[32,2,8,576]{3,2,1,0:T(8,128)(2,1)} %broadcast_in_dim.41), calls=%async_computation | async-start | bytes 1310720 | tf_op jit(solution)/shard_map/all_to_all | solution.py:34
  19.4 0.7 broadcast_add_fusion.1
  20.1 0.1 broadcast_add_fusion
  20.2 0.1 broadcast_compare_fusion
  20.3 15.5 %all-to-all-done = bf16[32,2,8,576]{3,2,1,0:T(8,128)(2,1)S(1)} async-done(((bf16[32,2,8,576]{3,2,1,0:T(8,128)(2,1)}), bf16[32,2,8,576]{3,2,1,0:T(8,128)(2,1)S(1)}, u32[]{:S(2)}, u32[]{:S(2)}) %all-to-all-start) | async-done | bytes 589856 | tf_op jit(solution)/shard_map/all_to_all | solution.py:34
  35.8 6.2 %fusion.6 = (bf16[2,32,8]{2,1,0:T(8,128)(2,1)S(1)}, f32[2,32,8,2048]{3,2,1,0:T(8,128)}) fusion(pred[2,8,2048]{2,1,0:T(8,128)(4,1)S(1)} %broadcast_compare_fusion, bf16[2,2048,576]{1,2,0:T(8,128)(2,1)} %param.6, bf16[32,2,8,576]{3,2,1,0:T(8,128)(2,1)S(1)} %all-to-all-done), kind=kOutput, calls=%fused_computation.9 | convolution fusion | flops 1211104768 | bytes 9536512 | tf_op jit(solution)/shard_map/sbrk,bpk->bsrp/dot_general | solution.py:38
  42.0 0.1 copy.46
  42.1 0.1 copy.47
  42.2 3.3 %fusion.9 = f32[2,32,8]{2,1,0:T(8,128)S(1)} fusion(f32[2,32,8,2048]{3,2,1,0:T(8,128)} %get-tuple-element.8, f32[2,32,8]{2,1,0:T(8,128)S(1)} %copy.47, pred[2,8,2048]{2,1,0:T(8,128)(4,1)S(1)} %broadcast_compare_fusion), kind=kLoop, calls=%fused_computation.12 | loop fusion | flops 5242368 | bytes 4231168 | tf_op jit(solution)/shard_map/reduce_sum | solution.py:46
  45.5 0.1 copy.49
  45.6 0.2 copy.50
  45.8 4.9 %fusion.18 = bf16[2,32,8,512]{3,2,1,0:T(8,128)(2,1)S(1)} fusion(bf16[2,2048,576]{1,2,0:T(8,128)(2,1)} %param.6, f32[2,32,8,2048]{3,2,1,0:T(8,128)} %get-tuple-element.8, f32[2,32,8]{2,1,0:T(8,128)S(1)} %copy.47, pred[2,8,2048]{2,1,0:T(8,128)(4,1)S(1)} %broadcast_compare_fusion), kind=kOutput, calls=%fused_computation.21 | convolution fusion | flops 1079246848 | bytes 8947712 | tf_op jit(solution)/shard_map/bsrp,bpl->bsrl/dot_general | solution.py:47
  50.7 0.1 fusion.28
  50.8 0.9 copy.51
  51.7 8.5 %all-to-all-start.1 = ((bf16[32,2,8,640]{3,2,1,0:T(8,128)(2,1)}), bf16[32,2,8,640]{3,2,1,0:T(8,128)(2,1)}, u32[]{:S(2)}, u32[]{:S(2)}) async-start(bf16[32,2,8,640]{3,2,1,0:T(8,128)(2,1)} %copy.51), calls=%async_computation.1 | async-start | bytes 1310720 | tf_op jit(solution)/shard_map/all_to_all | solution.py:58
  60.2 0.0 copy-done
  60.3 5.6 %collective-permute-start = (bf16[2,512,128]{2,1,0:T(8,128)(2,1)S(1)}, bf16[2,512,128]{2,1,0:T(8,128)(2,1)}, u32[]{:S(2)}, u32[]{:S(2)}) collective-permute-start(bf16[2,512,128]{2,1,0:T(8,128)(2,1)S(1)} %constant_dynamic-slice_fusion), channel_id=1, source_target_pairs={{0,0},{32,1},{64,2},{96,3},{128,4},{160,5},{192,6},{224,7},{256,8}... | collective-permute-start | bytes 786440 | tf_op jit(solution)/shard_map/ppermute | solution.py:31
  65.8 11.1 %all-to-all-done.1 = bf16[32,2,8,640]{3,2,1,0:T(8,128)(2,1)} async-done(((bf16[32,2,8,640]{3,2,1,0:T(8,128)(2,1)}), bf16[32,2,8,640]{3,2,1,0:T(8,128)(2,1)}, u32[]{:S(2)}, u32[]{:S(2)}) %all-to-all-start.1) | async-done | bytes 655392 | tf_op jit(solution)/shard_map/all_to_all | solution.py:58
  76.9 4.0 %copy.52 = bf16[32,2,8,640]{0,2,3,1:T(8,128)(2,1)S(1)} copy(bf16[32,2,8,640]{3,2,1,0:T(8,128)(2,1)} %all-to-all-done.1) | data formatting | bytes 1310720 | tf_op jit(solution)/shard_map/all_to_all | solution.py:58
  80.9 0.3 convert_element_type.89
  81.3 0.1 slice_reduce_fusion
  81.4 0.1 exponential_bitcast_fusion
  81.5 1.2 fusion.2
  82.6 0.2 fusion.34
  82.8 0.1 copy.62
  82.9 0.2 copy.54
  83.0 0.1 divide_convert_fusion
  83.1 0.0 collective-permute-done
  83.2 1.1 fusion.26
  84.3 0.1 broadcast_in_dim.44
  84.3 34.3 %all_to_all.15 = bf16[32,2,4,2,128]{4,3,2,1,0:T(2,128)(2,1)S(1)} all-to-all(bf16[32,2,4,2,128]{4,3,2,1,0:T(2,128)(2,1)S(1)} %broadcast_in_dim.44), channel_id=1, replica_groups=mesh['seq'=32,'batch'=16] {'seq'}, dimensions={0} | all-to-all | bytes 262144 | tf_op jit(solution)/shard_map/all_to_all | solution.py:67
  118.6 0.1 copy.58
  118.8 0.0 all-gather.2.cloned.1.call-done
  118.8 3.7 %fusion.23 = bf16[2,4,224]{2,1,0:T(4,128)(2,1)} fusion(bf16[2,4,8192]{2,1,0:T(4,128)(2,1)S(1)} %reshape.119, bf16[8192,224]{0,1:T(8,128)(2,1)} %all-gather.2.cloned.1.call-done), kind=kOutput, calls=%fused_computation.22 | convolution fusion | flops 29361920 | bytes 3804672 | tf_op jit(solution)/shard_map/btk,kd->btd/dot_general | solution.py:71
  (7 shorter events, 0.1 us)
Async XLA Ops:
  6.5 53.7 %copy-start = (bf16[4,512,128]{2,1,0:T(8,128)(2,1)S(1)}, bf16[4,512,128]{2,1,0:T(8,128)(2,1)}, u32[]{:S(2)}) copy-start(bf16[4,512,128]{2,1,0:T(8,128)(2,1)} %param.8) | copy-start | bytes 1572868
  6.5 112.3 %all-gather.2.cloned.1.call-start = ((), (), s32[]{:S(2)}) async-start(), calls=%async_computation.3 | async-start | bytes 3899392 | tf_op jit(solution)/shard_map/all_gather | solution.py:22
  8.9 26.9 %all-to-all-start = ((bf16[32,2,8,576]{3,2,1,0:T(8,128)(2,1)}), bf16[32,2,8,576]{3,2,1,0:T(8,128)(2,1)S(1)}, u32[]{:S(2)}, u32[]{:S(2)}) async-start(bf16[32,2,8,576]{3,2,1,0:T(8,128)(2,1)} %broadcast_in_dim.41), calls=%async_computation | async-start | bytes 1310720 | tf_op jit(solution)/shard_map/all_to_all | solution.py:34
  51.7 25.3 %all-to-all-start.1 = ((bf16[32,2,8,640]{3,2,1,0:T(8,128)(2,1)}), bf16[32,2,8,640]{3,2,1,0:T(8,128)(2,1)}, u32[]{:S(2)}, u32[]{:S(2)}) async-start(bf16[32,2,8,640]{3,2,1,0:T(8,128)(2,1)} %copy.51), calls=%async_computation.1 | async-start | bytes 1310720 | tf_op jit(solution)/shard_map/all_to_all | solution.py:58
  60.3 22.9 %collective-permute-start = (bf16[2,512,128]{2,1,0:T(8,128)(2,1)S(1)}, bf16[2,512,128]{2,1,0:T(8,128)(2,1)}, u32[]{:S(2)}, u32[]{:S(2)}) collective-permute-start(bf16[2,512,128]{2,1,0:T(8,128)(2,1)S(1)} %constant_dynamic-slice_fusion), channel_id=1, source_target_pairs={{0,0},{32,1},{64,2},{96,3},{128,4},{160,5},{192,6},{224,7},{256,8}... | collective-permute-start | bytes 786440 | tf_op jit(solution)/shard_map/ppermute | solution.py:31
Sparse Core Ops, SparseCore 0:
  9.5 50.8 all-gather.1

commit v2 on v0

v2 whole, which is shorter than its diff:
```python
import functools

import jax
import jax.numpy as jnp
from jax import lax
from jax.experimental import pallas as pl
from jax.experimental.pallas import tpu as pltpu
from jax.sharding import Mesh
from jax.sharding import PartitionSpec as P

ROPE = 64
NOPE = 128


NEG = -1e30
LANES = 128
CHUNKS = 8
VMEM = pl.BlockSpec(memory_space=pltpu.VMEM)
SMEM = pl.BlockSpec(memory_space=pltpu.SMEM)


def split(value, pieces):
    out = []
    for _ in range(pieces):
        piece = value.astype(jnp.bfloat16).astype(jnp.float32)
        out.append(piece)
        value = value - piece
    return out


def spread_kernel(scalars_ref, q_ref, out_ref):
    del scalars_ref
    seqs, ahead, own, width = q_ref.shape
    whole = width // LANES
    rest = []
    for b in range(seqs):
        rows = [q_ref[b, t, h : h + 1].astype(jnp.float32) for h in range(own) for t in range(ahead)]
        rows = jnp.concatenate(rows, axis=0)
        for c in range(whole):
            block = rows[:, c * LANES : (c + 1) * LANES].astype(out_ref.dtype)
            out_ref[:, b * whole + c] = jnp.broadcast_to(block[None], out_ref.shape[:1] + block.shape)
        rest.append(rows[:, whole * LANES :])
    rest = jnp.concatenate(rest, axis=1).astype(out_ref.dtype)
    out_ref[:, seqs * whole] = jnp.broadcast_to(rest[None], out_ref.shape[:1] + rest.shape)


def attend_kernel(own, ahead, scalars_ref, q_ref, keys_ref, out_ref):
    n_seq, _, rows, _ = q_ref.shape
    seqs, width, ctx_dev = keys_ref.shape
    whole, left = width // LANES, width % LANES
    latent = (out_ref.shape[2] - 1) * LANES
    all_rows = n_seq * rows
    scale = 1.0 / (NOPE + ROPE) ** 0.5
    base2 = scale * 1.4426950408889634
    row = lax.broadcasted_iota(jnp.int32, (all_rows, 1), 0)
    step = lax.rem(row, ahead)
    position = lax.broadcasted_iota(jnp.int32, (all_rows, ctx_dev), 1)
    lane = lax.broadcasted_iota(jnp.int32, (all_rows, LANES), 1)
    shift = scalars_ref[seqs + 1]
    scores = []
    for b in range(seqs):
        blocks = [q_ref[:, b * whole + c].reshape(all_rows, LANES) for c in range(whole)]
        rest = q_ref[:, seqs * whole].reshape(all_rows, LANES)
        queries = jnp.concatenate(blocks + [rest[:, b * left : (b + 1) * left]], axis=1)
        scores.append(jnp.dot(queries, keys_ref[b], preferred_element_type=jnp.float32))
    for b in range(seqs):
        limit = scalars_ref[b] - ahead + 1 - scalars_ref[seqs] + step
        masked = jnp.where(position < limit, scores[b], NEG)
        top = jnp.max(masked, axis=1, keepdims=True)
        weights = jnp.exp2((masked - jnp.maximum(top, 0.1 * NEG)) * base2)
        total = jnp.sum(weights, axis=1, keepdims=True)
        out = lax.dot_general(
            weights.astype(jnp.bfloat16),
            keys_ref[b, :latent],
            (((1,), (1,)), ((), ())),
            preferred_element_type=jnp.float32,
        )
        extra = jnp.zeros((all_rows, LANES), jnp.float32)
        for at, piece in enumerate(split(top * scale, 3) + split(total, 2)):
            extra = jnp.where(lane == at, piece, extra)
        out = out.astype(jnp.bfloat16)
        extra = extra.astype(jnp.bfloat16)
        for p in range(n_seq):
            owner = lax.rem(p + shift, n_seq)
            pair = slice(p * rows, (p + 1) * rows)
            for c in range(latent // LANES):
                out_ref[owner, b, c] = out[pair, c * LANES : (c + 1) * LANES]
            out_ref[owner, b, latent // LANES] = extra[pair]


def combine_kernel(own, ahead, parts_ref, up_ref, out_ref):
    n_seq, seqs, blocks, rows, _ = parts_ref.shape
    attended = []
    for b in range(seqs):
        extra = parts_ref[:, b, blocks - 1].astype(jnp.float32)
        top = extra[:, :, 0:1] + extra[:, :, 1:2] + extra[:, :, 2:3]
        total = extra[:, :, 3:4] + extra[:, :, 4:5]
        factor = jnp.exp(top - jnp.max(top, axis=0, keepdims=True))
        total = jnp.sum(total * factor, axis=0)
        latents = []
        for c in range(blocks - 1):
            latents.append(jnp.sum(parts_ref[:, b, c].astype(jnp.float32) * factor, axis=0) / total)
        attended.append(jnp.concatenate(latents, axis=1))
    values = []
    for h in range(own):
        mine = [one[h * ahead : (h + 1) * ahead] for one in attended]
        mine = jnp.concatenate(mine + mine, axis=0).astype(jnp.bfloat16)
        one = jnp.dot(mine, up_ref[h], preferred_element_type=jnp.float32)
        values.append(one[: seqs * ahead])
    values = jnp.concatenate(values, axis=0).astype(jnp.bfloat16)
    out_ref[...] = jnp.broadcast_to(values[None], out_ref.shape)


def project_kernel(own, shift_ref, values_ref, weight_ref, out_ref):
    n_seq, rows, vdim = values_ref.shape
    seqs, ahead, _ = out_ref.shape
    columns = weight_ref.shape[0]
    depth = weight_ref.shape[1] // CHUNKS
    steps = rows // own
    pairs = depth // (own * vdim)
    row = lax.broadcasted_iota(jnp.int32, (rows, 1), 0)
    kept = [row // steps == h for h in range(own)]
    out = jnp.zeros((rows, columns), jnp.float32)
    for k in range(CHUNKS):
        flat = []
        for p in range(pairs):
            owner = lax.rem(k * pairs + p + shift_ref[0], n_seq)
            value = values_ref[owner].astype(jnp.float32)
            flat += [jnp.where(one, value, 0.0).astype(jnp.bfloat16) for one in kept]
        out += lax.dot_general(
            jnp.concatenate(flat, axis=1),
            weight_ref[:, k * depth : (k + 1) * depth],
            (((1,), (1,)), ((), ())),
            preferred_element_type=jnp.float32,
        )
    out = sum(out[h * steps : (h + 1) * steps] for h in range(own)).astype(out_ref.dtype)
    for b in range(seqs):
        out_ref[b] = out[b * ahead : (b + 1) * ahead]


def call(kernel, shape, dtype, specs, *operands, scratch=(), limit=24):
    return pl.pallas_call(
        kernel,
        out_shape=jax.ShapeDtypeStruct(shape, dtype),
        in_specs=specs,
        out_specs=VMEM,
        scratch_shapes=scratch,
        compiler_params=pltpu.CompilerParams(vmem_limit_bytes=limit * 1024 * 1024),
    )(*operands)


def per_device(query, cache, lengths, value_up, out_weight):
    n_seq = lax.axis_size("seq")
    chips, cores = lax.axis_size("z"), lax.axis_size("core")
    n_batch = chips * cores
    seqs, ahead, own, width = query.shape
    ctx_dev = cache.shape[1]
    held, latent, vdim = value_up.shape
    seq = lax.axis_index("seq")
    group = lax.axis_index("z") * cores + lax.axis_index("core")
    rows = ahead * own
    bf16 = jnp.bfloat16
    per_group = held // own
    shift = (per_group * group).astype(jnp.int32).reshape(1)

    scalars = jnp.concatenate([lengths, (seq * ctx_dev).astype(jnp.int32).reshape(1), shift])
    queries = call(spread_kernel, (n_seq, seqs * width // LANES, rows, LANES), bf16, [SMEM, VMEM], scalars, query)
    queries = lax.all_to_all(queries, "seq", 0, 0, tiled=True)

    weight = lax.all_gather(out_weight, ("z", "core"), axis=0, tiled=True).T
    mine = lax.dynamic_slice_in_dim(value_up, lax.rem(seq, per_group) * own, own, 0)
    pairs = []
    for s in range(n_seq):
        for g in range(n_batch):
            pairs.append((s * n_batch + (s // per_group - g) % n_batch, s * n_batch + g))
    up = lax.ppermute(mine, ("seq", "z", "core"), pairs)

    parts = call(
        functools.partial(attend_kernel, own, ahead),
        (n_seq, seqs, latent // LANES + 1, rows, LANES),
        bf16,
        [SMEM, VMEM, VMEM],
        scalars,
        queries,
        cache.swapaxes(1, 2),
    )
    parts = lax.all_to_all(parts, "seq", 0, 0, tiled=True)
    values = call(
        functools.partial(combine_kernel, own, ahead),
        (n_seq, seqs * rows, vdim),
        bf16,
        [VMEM, VMEM],
        parts,
        up,
    )
    values = lax.all_to_all(values, "seq", 0, 0, tiled=True)
    return call(
        functools.partial(project_kernel, own),
        (seqs, ahead, out_weight.shape[1]),
        bf16,
        [SMEM, VMEM, VMEM],
        shift,
        values,
        weight,
    )


def solution(mesh):
    n_seq, n_batch = mesh.devices.shape
    split_mesh = Mesh(mesh.devices.reshape(n_seq, n_batch // 2, 2), ("seq", "z", "core"))
    batch = ("z", "core")
    placed = (
        P(batch, None, "seq", None),
        P(batch, "seq", None),
        P(batch),
        P(batch, None, None),
        P(batch, "seq"),
    )
    return jax.shard_map(
        per_device, mesh=split_mesh, in_specs=placed, out_specs=P(batch, None, "seq"), check_vma=False
    )
```

time: 385 us -> 102 us (0.26)
  blocking collectives: 198 us -> 42.2 us
  waiting for transfers between devices: 138 us -> 12.8 us
  matrix products: 11.3 us -> 0 us
  Pallas kernels: 0 us -> 7.97 us
  starting transfers between devices: 12.6 us -> 18.5 us
  other arithmetic: 5.9 us -> 0.73 us
    psum x1 -> x0, waiting for transfers between devices: 122 us -> none  [per_device(): lax.psum((block_total * factor, block_out * factor[..., None]), 'seq')]
    pmax x1 -> x0, blocking collectives: 58.1 us -> none  [per_device(): top = lax.pmax(block_top, 'seq')]
    psum x1 -> x0, blocking collectives: 56.1 us -> none  [per_device(): lax.psum((block_total * factor, block_out * factor[..., None]), 'seq')]
    unnamed x1 -> x0, blocking collectives: 43.4 us -> none
    all_to_all x0 -> x2, blocking collectives: none -> 42.2 us  [the longest x1 25.6 us: per_device(): queries = lax.all_to_all(queries, 'seq', 0, 0, tiled=True)]
    all_gather x1 -> x0, blocking collectives: 39.9 us -> none  [per_device(): queries = lax.all_gather(query, 'seq', axis=2, tiled=True)]
    all_to_all x1, waiting for transfers between devices: 15.4 us -> 0.01 us  [per_device(): parts = lax.all_to_all(parts, 'seq', 0, 0, tiled=True)]
    ppermute x0 -> x1, waiting for transfers between devices: none -> 12.1 us  [per_device(): up = lax.ppermute(mine, ('seq', 'z', 'core'), pairs)]
  transfers between devices with their start and end apart: 2 -> 3, of which waited for: 2 -> 1; matrix products, arithmetic and copies ran while one was open for 0% -> 1% of each run, Pallas kernels for 0% -> 6%
where the time goes in v2:
time: 102 us; the launch traced here: 101 us
  blocking collectives  42.2 us (41%)
  starting transfers between devices  18.5 us (18%)
  between operations  13.5 us (13%)
  waiting for transfers between devices  12.8 us (13%)
  Pallas kernels  7.97 us (8%)
  local copies, waits for them, and re-layouts  5.25 us (5%)
    all_to_all x1, blocking collectives, per_device(): queries = lax.all_to_all(queries, 'seq', 0, 0, tiled=True)  25.6 us
    all_to_all x1, blocking collectives, per_device(): values = lax.all_to_all(values, 'seq', 0, 0, tiled=True)  16.6 us
    ppermute x1, waiting for transfers between devices, per_device(): up = lax.ppermute(mine, ('seq', 'z', 'core'), pairs)  12.1 us
    ppermute x1, starting transfers between devices, per_device(): up = lax.ppermute(mine, ('seq', 'z', 'core'), pairs)  10.6 us
    pallas_call x4, Pallas kernels, call(): pl.pallas_call(kernel, out_shape=jax.ShapeDtypeStruct(shape, dtype), in_s...  7.97 us
    all_to_all x1, starting transfers between devices, per_device(): parts = lax.all_to_all(parts, 'seq', 0, 0, tiled=True)  7.83 us
    unnamed x8, local copies, waits for them, and re-layouts  5.22 us
  transfers between devices with their start and end apart: 3, of which 1 were waited for; matrix products, arithmetic and copies ran while one was open for 1% of the time, Pallas kernels for 6%

profile of v2, /device:TPU:1, one launch (start us, length us, event | category | flops | bytes accessed | tf_op | source)
XLA Modules:
  0.0 100.8 jit_solution(4001873480940036919)
XLA Ops:
  6.5 0.0 copy-start
  6.5 0.0 all-gather.2.cloned.1.call-start
  6.5 0.7 all-gather.2.cloned.1.call-update
  7.3 0.7 pad_add_fusion.scalars_ref
  8.0 0.0 copy-start.3
  8.0 0.7 copy-done.3
  8.7 0.7 shard_map.55
  9.4 25.6 %all_to_all.15.q_ref = bf16[32,9,8,128]{3,2,1,0:T(8,128)(2,1)S(1)} all-to-all(bf16[32,9,8,128]{3,2,1,0:T(8,128)(2,1)S(1)} %shard_map.55), channel_id=1, replica_groups=mesh['seq'=32,'z'=8,'core'=2] {'seq'}, dimensions={0} | all-to-all | bytes 1179648 | tf_op jit(solution)/shard_map/all_to_all | solution.py:168
  35.0 0.0 copy-start.1
  35.0 2.4 %copy-done.1 = bf16[2,2048,576]{1,2,0:T(8,128)(2,1)S(1)} copy-done((bf16[2,2048,576]{1,2,0:T(8,128)(2,1)S(1)}, bf16[2,2048,576]{1,2,0:T(8,128)(2,1)}, u32[]{:S(2)}) %copy-start.1) | copy-done | bytes 4718616
  37.4 5.1 %shard_map.56 = bf16[32,2,5,8,128]{4,3,2,1,0:T(8,128)(2,1)} custom-call(s32[4]{0:T(128)S(1)} %pad_add_fusion.scalars_ref, bf16[32,9,8,128]{3,2,1,0:T(8,128)(2,1)S(1)} %all_to_all.15.q_ref, bf16[2,576,2048]{2,1,0:T(8,128)(2,1)S(1)} %bitcast.4), custom_call_target="tpu_custom_call" | custom-call | tf_op jit(solution)/shard_map/pallas_call | solution.py:142
  42.5 7.8 %all-to-all-start.1 = ((bf16[32,2,5,8,128]{4,3,2,1,0:T(8,128)(2,1)}), bf16[32,2,5,8,128]{4,3,2,1,0:T(8,128)(2,1)S(1)}, u32[]{:S(2)}, u32[]{:S(2)}) async-start(bf16[32,2,5,8,128]{4,3,2,1,0:T(8,128)(2,1)} %shard_map.56), calls=%async_computation.1 | async-start | bytes 1310720 | tf_op jit(solution)/shard_map/all_to_all | solution.py:187
  50.4 0.0 copy-done
  50.4 10.6 %collective-permute-start = (bf16[2,512,128]{2,1,0:T(8,128)(2,1)S(1)}, bf16[2,512,128]{2,1,0:T(8,128)(2,1)S(1)}, u32[]{:S(2)}, u32[]{:S(2)}) collective-permute-start(bf16[2,512,128]{2,1,0:T(8,128)(2,1)S(1)} %constant_dynamic-slice_fusion), channel_id=1, source_target_pairs={{0,0},{15,1},{14,2},{13,3},{12,4},{11,5},{10,6},{9,7},{8,8},{7,9},... | collective-permute-start | bytes 786440 | tf_op jit(solution)/shard_map/ppermute | solution.py:176
  61.1 12.1 %collective-permute-done.up_ref = bf16[2,512,128]{2,1,0:T(8,128)(2,1)S(1)} collective-permute-done((bf16[2,512,128]{2,1,0:T(8,128)(2,1)S(1)}, bf16[2,512,128]{2,1,0:T(8,128)(2,1)S(1)}, u32[]{:S(2)}, u32[]{:S(2)}) %collective-permute-start) | collective-permute-done | bytes 262176 | tf_op jit(solution)/shard_map/ppermute | solution.py:176
  73.1 0.0 all-to-all-done.1.parts_ref
  73.2 0.5 shard_map.57
  73.7 16.6 %all_to_all.16.values_ref = bf16[32,16,128]{2,1,0:T(8,128)(2,1)S(1)} all-to-all(bf16[32,16,128]{2,1,0:T(8,128)(2,1)S(1)} %shard_map.57), channel_id=1, replica_groups=mesh['seq'=32,'z'=8,'core'=2] {'seq'}, dimensions={0} | all-to-all | bytes 262144 | tf_op jit(solution)/shard_map/all_to_all | solution.py:196
  90.3 0.0 all-gather.2.cloned.1.call-done
  90.3 0.0 copy-start.2
  90.3 2.0 %copy-done.2 = bf16[8192,224]{0,1:T(8,128)(2,1)S(1)} copy-done((bf16[8192,224]{0,1:T(8,128)(2,1)S(1)}, bf16[8192,224]{0,1:T(8,128)(2,1)}, u32[]{:S(2)}) %copy-start.2) | copy-done | bytes 3670040
  92.3 1.7 %shard_map.58 = bf16[2,4,224]{2,1,0:T(4,128)(2,1)} custom-call(s32[1]{0:T(128)} %bitcast.shift_ref, bf16[32,16,128]{2,1,0:T(8,128)(2,1)S(1)} %all_to_all.16.values_ref, bf16[224,8192]{1,0:T(8,128)(2,1)S(1)} %bitcast.5), custom_call_target="tpu_custom_call" | custom-call | tf_op jit(solution)/shard_map/pallas_call | solution.py:142
  (1 shorter events, 0.0 us)
Async XLA Ops:
  6.5 43.9 %copy-start = (bf16[4,512,128]{2,1,0:T(8,128)(2,1)S(1)}, bf16[4,512,128]{2,1,0:T(8,128)(2,1)}, u32[]{:S(2)}) copy-start(bf16[4,512,128]{2,1,0:T(8,128)(2,1)} %param.8) | copy-start | bytes 1572868
  6.5 83.7 %all-gather.2.cloned.1.call-start = ((), (), s32[]{:S(2)}) async-start(), calls=%async_computation.3 | async-start | bytes 3899392 | tf_op jit(solution)/shard_map/all_gather | solution.py:170
  8.0 0.7 copy-start.3
  35.0 2.5 %copy-start.1 = (bf16[2,2048,576]{1,2,0:T(8,128)(2,1)S(1)}, bf16[2,2048,576]{1,2,0:T(8,128)(2,1)}, u32[]{:S(2)}) copy-start(bf16[2,2048,576]{1,2,0:T(8,128)(2,1)} %param.6) | copy-start | bytes 14155780
  42.5 30.6 %all-to-all-start.1 = ((bf16[32,2,5,8,128]{4,3,2,1,0:T(8,128)(2,1)}), bf16[32,2,5,8,128]{4,3,2,1,0:T(8,128)(2,1)S(1)}, u32[]{:S(2)}, u32[]{:S(2)}) async-start(bf16[32,2,5,8,128]{4,3,2,1,0:T(8,128)(2,1)} %shard_map.56), calls=%async_computation.1 | async-start | bytes 1310720 | tf_op jit(solution)/shard_map/all_to_all | solution.py:187
  50.4 22.7 %collective-permute-start = (bf16[2,512,128]{2,1,0:T(8,128)(2,1)S(1)}, bf16[2,512,128]{2,1,0:T(8,128)(2,1)S(1)}, u32[]{:S(2)}, u32[]{:S(2)}) collective-permute-start(bf16[2,512,128]{2,1,0:T(8,128)(2,1)S(1)} %constant_dynamic-slice_fusion), channel_id=1, source_target_pairs={{0,0},{15,1},{14,2},{13,3},{12,4},{11,5},{10,6},{9,7},{8,8},{7,9},... | collective-permute-start | bytes 786440 | tf_op jit(solution)/shard_map/ppermute | solution.py:176
  90.3 2.0 %copy-start.2 = (bf16[8192,224]{0,1:T(8,128)(2,1)S(1)}, bf16[8192,224]{0,1:T(8,128)(2,1)}, u32[]{:S(2)}) copy-start(bf16[8192,224]{0,1:T(8,128)(2,1)} %all-gather.2.cloned.1.call-done) | copy-start | bytes 11010052
Sparse Core Ops, SparseCore 0:
  9.5 50.8 all-gather.1

commit v3 on v2

v3 whole, which is shorter than its diff:
```python
import functools

import jax
import jax.numpy as jnp
from jax import lax
from jax.experimental import pallas as pl
from jax.experimental.pallas import tpu as pltpu
from jax.sharding import Mesh
from jax.sharding import PartitionSpec as P

ROPE = 64
NOPE = 128


NEG = -1e30
LANES = 128
PARTS = 4
PIECES = 5
VMEM = pl.BlockSpec(memory_space=pltpu.VMEM)
HBM = pl.BlockSpec(memory_space=pltpu.HBM)
SMEM = pl.BlockSpec(memory_space=pltpu.SMEM)


def owner_of(pair, n_seq, chips, start, core):
    at_chip = n_seq // chips
    half = at_chip // 2
    chip, rest = lax.div(pair, at_chip), lax.rem(pair, at_chip)
    swapped = lax.rem(lax.div(rest, half) + core, 2)
    return lax.rem(chip + start, chips) * at_chip + swapped * half + lax.rem(rest, half)


def split(value, pieces):
    out = []
    for _ in range(pieces):
        piece = value.astype(jnp.bfloat16).astype(jnp.float32)
        out.append(piece)
        value = value - piece
    return out


def spread_kernel(q_ref, out_ref):
    seqs, ahead, own, width = q_ref.shape
    whole = width // LANES
    rest = []
    for b in range(seqs):
        rows = [q_ref[b, t, h : h + 1].astype(jnp.float32) for h in range(own) for t in range(ahead)]
        rows = jnp.concatenate(rows, axis=0)
        for c in range(whole):
            block = rows[:, c * LANES : (c + 1) * LANES].astype(out_ref.dtype)
            out_ref[:, b * whole + c] = jnp.broadcast_to(block[None], out_ref.shape[:1] + block.shape)
        rest.append(rows[:, whole * LANES :])
    rest = jnp.concatenate(rest, axis=1).astype(out_ref.dtype)
    out_ref[:, seqs * whole] = jnp.broadcast_to(rest[None], out_ref.shape[:1] + rest.shape)


def attend_kernel(own, ahead, chips, scalars_ref, q_ref, cache_ref, up_ref, out_ref, keys_ref, sems):
    del up_ref
    n_seq, _, rows, _ = q_ref.shape
    seqs, width, ctx_dev = keys_ref.shape
    whole, left = width // LANES, width % LANES
    latent = (out_ref.shape[1] - 1) // seqs * LANES
    all_rows = n_seq * rows
    scale = 1.0 / (NOPE + ROPE) ** 0.5
    base2 = scale * 1.4426950408889634
    row = lax.broadcasted_iota(jnp.int32, (all_rows, 1), 0)
    step = lax.rem(row, ahead)
    position = lax.broadcasted_iota(jnp.int32, (all_rows, ctx_dev), 1)
    lane = lax.broadcasted_iota(jnp.int32, (all_rows, LANES), 1)
    start, core = scalars_ref[seqs + 1], scalars_ref[seqs + 2]
    part = ctx_dev // PARTS
    copies = {}
    for b in range(seqs):
        for k in range(PARTS):
            at = pl.ds(k * part, part)
            copies[b, k] = pltpu.make_async_copy(
                cache_ref.at[b, :, at], keys_ref.at[b, :, at], sems.at[b, k]
            )
    for k in range(PARTS):
        copies[0, k].start()
    extra = jnp.zeros((all_rows, LANES), jnp.float32)
    for b in range(seqs):
        blocks = [q_ref[:, b * whole + c].reshape(all_rows, LANES) for c in range(whole)]
        rest = q_ref[:, seqs * whole].reshape(all_rows, LANES)
        queries = jnp.concatenate(blocks + [rest[:, b * left : (b + 1) * left]], axis=1)
        scores = []
        for k in range(PARTS):
            copies[b, k].wait()
            if b + 1 < seqs:
                copies[b + 1, k].start()
            keys = keys_ref[b, :, k * part : (k + 1) * part]
            scores.append(jnp.dot(queries, keys, preferred_element_type=jnp.float32))
        scores = jnp.concatenate(scores, axis=1)
        limit = scalars_ref[b] - ahead + 1 - scalars_ref[seqs] + step
        masked = jnp.where(position < limit, scores, NEG)
        top = jnp.max(masked, axis=1, keepdims=True)
        weights = jnp.exp2((masked - jnp.maximum(top, 0.1 * NEG)) * base2)
        total = jnp.sum(weights, axis=1, keepdims=True)
        out = lax.dot_general(
            weights.astype(jnp.bfloat16),
            keys_ref[b, :latent],
            (((1,), (1,)), ((), ())),
            preferred_element_type=jnp.float32,
        )
        for at, piece in enumerate(split(top * scale, 3) + split(total, 2)):
            extra = jnp.where(lane == PIECES * b + at, piece, extra)
        out = out.astype(jnp.bfloat16)
        for p in range(n_seq):
            owner = owner_of(p, n_seq, chips, start, core)
            for c in range(latent // LANES):
                block = out[p * rows : (p + 1) * rows, c * LANES : (c + 1) * LANES]
                out_ref[owner, b * (latent // LANES) + c] = block
    extra = extra.astype(jnp.bfloat16)
    for p in range(n_seq):
        owner = owner_of(p, n_seq, chips, start, core)
        out_ref[owner, seqs * (latent // LANES)] = extra[p * rows : (p + 1) * rows]


def combine_kernel(own, ahead, parts_ref, up_ref, out_ref):
    n_seq, blocks, rows, _ = parts_ref.shape
    seqs = out_ref.shape[1] // rows
    each = (blocks - 1) // seqs
    extra = parts_ref[:, blocks - 1].astype(jnp.float32)
    attended = []
    for b in range(seqs):
        piece = [extra[:, :, PIECES * b + k : PIECES * b + k + 1] for k in range(PIECES)]
        top = piece[0] + piece[1] + piece[2]
        total = piece[3] + piece[4]
        factor = jnp.exp(top - jnp.max(top, axis=0, keepdims=True))
        total = jnp.sum(total * factor, axis=0)
        latents = []
        for c in range(each):
            latents.append(jnp.sum(parts_ref[:, each * b + c].astype(jnp.float32) * factor, axis=0) / total)
        attended.append(jnp.concatenate(latents, axis=1))
    values = []
    for h in range(own):
        mine = [one[h * ahead : (h + 1) * ahead] for one in attended]
        mine = jnp.concatenate(mine + mine, axis=0).astype(jnp.bfloat16)
        one = jnp.dot(mine, up_ref[h], preferred_element_type=jnp.float32)
        values.append(one[: seqs * ahead])
    values = jnp.concatenate(values, axis=0).astype(jnp.bfloat16)
    out_ref[...] = jnp.broadcast_to(values[None], out_ref.shape)


def project_kernel(own, chips, cores, place_ref, values_ref, *refs):
    *weight_refs, out_ref = refs
    _, n_seq, rows, vdim = values_ref.shape
    steps = rows // own
    pairs = n_seq // (chips * cores)
    row = lax.broadcasted_iota(jnp.int32, (cores * rows, 1), 0)
    kept = [lax.rem(row, rows) // steps == h for h in range(own)]
    chip, core = place_ref[0], place_ref[1]

    def term(weight, at, c):
        flat = []
        for p in range(pairs):
            pair = (at * cores + c) * pairs + p
            value = []
            for g in range(cores):
                start = lax.rem((chips - 3) * chip + chips // 2 * g, chips)
                value.append(values_ref[g, owner_of(pair, n_seq, chips, start, g)].astype(jnp.float32))
            value = jnp.concatenate(value, axis=0)
            flat += [jnp.where(one, value, 0.0).astype(jnp.bfloat16) for one in kept]
        return lax.dot_general(
            jnp.concatenate(flat, axis=1),
            weight,
            (((1,), (1,)), ((), ())),
            preferred_element_type=jnp.float32,
        )

    last = len(weight_refs) - 1
    out = term(weight_refs[0][...], chip, core)
    for k in range(1, last):
        at = lax.rem(jnp.where(core == 0, chip + chips - k, chip + k), chips)
        for c in range(cores):
            out += term(weight_refs[k][c], at, c)
    out += term(weight_refs[last][...], lax.rem(chip + last, chips), core)
    for g in range(cores):
        out_ref[g] = sum(out[g * rows + h * steps : g * rows + (h + 1) * steps] for h in range(own))


def exchange(blocks):
    flat = blocks.reshape(blocks.shape[0], -1, LANES)
    return lax.all_to_all(flat, "seq", 0, 0, tiled=True).reshape(blocks.shape)


def call(kernel, shape, dtype, specs, *operands, scratch=(), limit=24):
    return pl.pallas_call(
        kernel,
        out_shape=jax.ShapeDtypeStruct(shape, dtype),
        in_specs=specs,
        out_specs=VMEM,
        scratch_shapes=scratch,
        compiler_params=pltpu.CompilerParams(vmem_limit_bytes=limit * 1024 * 1024),
    )(*operands)


def per_device(query, cache, lengths, value_up, out_weight):
    n_seq = lax.axis_size("seq")
    chips, cores = lax.axis_size("z"), lax.axis_size("core")
    n_batch = chips * cores
    seqs, ahead, own, width = query.shape
    ctx_dev = cache.shape[1]
    held, latent, vdim = value_up.shape
    seq = lax.axis_index("seq")
    rows = ahead * own
    bf16 = jnp.bfloat16
    per_group = held // own
    z, core = lax.axis_index("z"), lax.axis_index("core")
    place = jnp.stack([lax.rem((chips - 3) * z + chips // 2 * core, chips), core]).astype(jnp.int32)
    scalars = jnp.concatenate([lengths, (seq * ctx_dev).astype(jnp.int32).reshape(1), place])

    blocks = seqs * (latent // LANES) + 1
    queries = call(spread_kernel, (n_seq, blocks, rows, LANES), bf16, [VMEM], query)
    queries = exchange(queries)

    ring = [
        (chip * cores + c, (chip + 1 - 2 * c) % chips * cores + c)
        for chip in range(chips)
        for c in range(cores)
    ]
    batch = ("z", "core")
    block = lax.all_gather(out_weight.T, "core")
    weights = [out_weight.T]
    for _ in range(chips // 2 - 1):
        block = lax.ppermute(block, batch, ring)
        weights.append(block)
    weights.append(lax.ppermute(lax.dynamic_index_in_dim(block, core, 0, False), batch, ring))
    mine = lax.dynamic_slice_in_dim(value_up, lax.rem(seq, per_group) * own, own, 0)
    pairs = []
    for s in range(n_seq):
        at, swap = s // (n_seq // chips), s // per_group % cores
        for to in range(chips):
            for c in range(cores):
                source = (3 * to + chips // 2 * c + at) % chips * cores + (c + swap) % cores
                pairs.append((s * n_batch + source, (s * chips + to) * cores + c))
    up = lax.ppermute(mine, ("seq", "z", "core"), pairs)

    parts = call(
        functools.partial(attend_kernel, own, ahead, chips),
        (n_seq, blocks, rows, LANES),
        bf16,
        [SMEM, VMEM, HBM, VMEM],
        scalars,
        queries,
        cache.swapaxes(1, 2),
        up[:, :16],
        scratch=[
            pltpu.VMEM((seqs, width, ctx_dev), bf16),
            pltpu.SemaphoreType.DMA((seqs, PARTS)),
        ],
        limit=52,
    )
    parts = exchange(parts)
    values = call(
        functools.partial(combine_kernel, own, ahead),
        (n_seq, seqs * rows, vdim),
        bf16,
        [VMEM, VMEM],
        parts,
        up,
    )
    values = exchange(values)
    terms = call(
        functools.partial(project_kernel, own, chips, cores),
        (cores, seqs * ahead, out_weight.shape[1]),
        jnp.float32,
        [SMEM, VMEM] + [VMEM] * len(weights),
        jnp.stack([z, core]).astype(jnp.int32),
        lax.all_gather(values, "core"),
        *weights,
    )
    terms = lax.all_gather(terms, "core")
    out = lax.dynamic_index_in_dim(terms, core, 1, False).sum(axis=0)
    return out.reshape(seqs, ahead, out_weight.shape[1]).astype(bf16)


def solution(mesh):
    n_seq, n_batch = mesh.devices.shape
    split_mesh = Mesh(mesh.devices.reshape(n_seq, n_batch // 2, 2), ("seq", "z", "core"))
    batch = ("z", "core")
    placed = (
        P(batch, None, "seq", None),
        P(batch, "seq", None),
        P(batch),
        P(batch, None, None),
        P(batch, "seq"),
    )
    return jax.shard_map(
        per_device, mesh=split_mesh, in_specs=placed, out_specs=P(batch, None, "seq"), check_vma=False
    )
```

time: 102 us -> 91.9 us (0.901)
  starting transfers between devices: 18.5 us -> 56.4 us
  blocking collectives: 42.2 us -> 7.86 us
  between operations: 13.5 us -> 0.16 us
  local copies, waits for them, and re-layouts: 5.25 us -> 1.45 us
  Pallas kernels: 7.97 us -> 10.9 us
    all_to_all x2 -> x0, blocking collectives: 42.2 us -> none  [the longest x1 25.6 us: per_device(): queries = lax.all_to_all(queries, 'seq', 0, 0, tiled=True)]
    all_to_all x1 -> x3, starting transfers between devices: 7.83 us -> 29.4 us  [exchange(): return lax.all_to_all(flat, 'seq', 0, 0, tiled=True).reshape(blocks.shape)]
    ppermute x0 -> x4, starting transfers between devices: none -> 16.4 us  [the longest x3 13.4 us: per_device(): block = lax.ppermute(block, batch, ring)]
    ppermute x1, waiting for transfers between devices: 12.1 us -> 0.01 us  [per_device(): up = lax.ppermute(mine, ('seq', 'z', 'core'), pairs)]
    all_to_all x1 -> x3, waiting for transfers between devices: 0.01 us -> 8.31 us  [exchange(): return lax.all_to_all(flat, 'seq', 0, 0, tiled=True).reshape(blocks.shape)]
    all_gather x0 -> x3, blocking collectives: none -> 7.86 us  [the longest x1 3.66 us: per_device(): lax.all_gather(values, 'core')]
    ppermute x0 -> x4, waiting for transfers between devices: none -> 5.41 us  [the longest x3 5.41 us: per_device(): block = lax.ppermute(block, batch, ring)]
    unnamed x8 -> x6, local copies, waits for them, and re-layouts: 5.22 us -> 0.79 us
  transfers between devices with their start and end apart: 3 -> 8, of which waited for: 1 -> 3; matrix products, arithmetic and copies ran while one was open for 1% -> 1% of each run, Pallas kernels for 6% -> 10%
where the time goes in v3:
time: 91.9 us; the launch traced here: 91.4 us
  starting transfers between devices  56.4 us (61%)
  waiting for transfers between devices  13.7 us (15%)
  Pallas kernels  10.9 us (12%)
  blocking collectives  7.86 us (9%)
  local copies, waits for them, and re-layouts  1.45 us (2%)
    all_to_all x3, starting transfers between devices, exchange(): return lax.all_to_all(flat, 'seq', 0, 0, tiled=True).reshape(blocks.shape)  29.4 us
    ppermute x3, starting transfers between devices, per_device(): block = lax.ppermute(block, batch, ring)  13.4 us
    pallas_call x4, Pallas kernels, call(): pl.pallas_call(kernel, out_shape=jax.ShapeDtypeStruct(shape, dtype), in_s...  10.9 us
    ppermute x1, starting transfers between devices, per_device(): up = lax.ppermute(mine, ('seq', 'z', 'core'), pairs)  10.6 us
    all_to_all x3, waiting for transfers between devices, exchange(): return lax.all_to_all(flat, 'seq', 0, 0, tiled=True).reshape(blocks.shape)  8.31 us
    ppermute x3, waiting for transfers between devices, per_device(): block = lax.ppermute(block, batch, ring)  5.41 us
    all_gather x1, blocking collectives, per_device(): lax.all_gather(values, 'core')  3.66 us
    ppermute x1, starting transfers between devices, per_device(): lax.ppermute(lax.dynamic_index_in_dim(block, core, 0, False), batch, ring)  2.98 us
  transfers between devices with their start and end apart: 8, of which 3 were waited for; matrix products, arithmetic and copies ran while one was open for 1% of the time, Pallas kernels for 10%

profile of v3, /device:TPU:1, one launch (start us, length us, event | category | flops | bytes accessed | tf_op | source)
XLA Modules:
  0.0 91.4 jit_solution(13314205040878684725)
XLA Ops:
  0.0 0.0 copy-start
  0.0 0.0 copy-start.2
  0.0 0.8 copy-done.2
  0.8 0.9 %shard_map.55 = bf16[32,9,8,128]{3,2,1,0:T(8,128)(2,1)} custom-call(bf16[2,4,2,576]{3,2,1,0:T(2,128)(2,1)S(1)} %copy-done.2), custom_call_target="tpu_custom_call" | custom-call | tf_op jit(solution)/shard_map/pallas_call | solution.py:187
  1.7 10.5 %all-to-all-start = ((bf16[32,72,128]{2,1,0:T(8,128)(2,1)}), bf16[32,72,128]{2,1,0:T(8,128)(2,1)S(1)}, u32[]{:S(2)}, u32[]{:S(2)}) async-start(bf16[32,72,128]{2,1,0:T(8,128)(2,1)} %bitcast.4), calls=%async_computation | async-start | bytes 1179648 | tf_op jit(solution)/shard_map/all_to_all | solution.py:183
  12.2 0.0 copy-done
  12.3 10.6 %collective-permute-start = (bf16[2,512,128]{2,1,0:T(8,128)(2,1)S(1)}, bf16[2,512,128]{2,1,0:T(8,128)(2,1)S(1)}, u32[]{:S(2)}, u32[]{:S(2)}) collective-permute-start(bf16[2,512,128]{2,1,0:T(8,128)(2,1)S(1)} %constant_dynamic-slice_fusion), channel_id=1, source_target_pairs={{0,0},{9,1},{6,2},{15,3},{12,4},{5,5},{2,6},{11,7},{8,8},{1,9},{14... | collective-permute-start | bytes 786440 | tf_op jit(solution)/shard_map/ppermute | solution.py:236
  22.9 2.3 %all-gather.1 = bf16[448,512]{1,0:T(8,128)(2,1)S(1)} all-gather(bf16[224,512]{1,0:T(8,128)(2,1)} %bitcast.18), channel_id=3, replica_groups=mesh['seq'=32,'z'=8,'core'=2] {'core'}, dimensions={0}, use_global_device_ids=true | all-gather | bytes 688128 | tf_op jit(solution)/shard_map/all_gather | solution.py:222
  25.3 0.0 copy-start.1
  25.3 3.2 %collective-permute-start.1 = (bf16[2,224,512]{2,1,0:T(8,128)(2,1)S(1)}, bf16[2,224,512]{2,1,0:T(8,128)(2,1)S(1)}, u32[]{:S(2)}, u32[]{:S(2)}) collective-permute-start(bf16[2,224,512]{2,1,0:T(8,128)(2,1)S(1)} %bitcast.21), channel_id=1, source_target_pairs={{0,2},{1,15},{2,4},{3,1},{4,6},{5,3},{6,8},{7,5},{8,10},{9,7},{10,... | collective-permute-start | bytes 1376264 | tf_op jit(solution)/shard_map/ppermute | solution.py:225
  28.5 0.7 pad_add_fusion.1.scalars_ref
  29.2 0.0 collective-permute-done.up_ref
  29.2 0.0 all-to-all-done
  29.2 7.6 %shard_map.56 = bf16[32,9,8,128]{3,2,1,0:T(8,128)(2,1)} custom-call(s32[5]{0:T(128)S(1)} %pad_add_fusion.1.scalars_ref, bf16[32,9,8,128]{3,2,1,0:T(8,128)(2,1)S(1)} %bitcast.15, bf16[2,576,2048]{2,1,0:T(8,128)(2,1)} %bitcast.20, bf16[2,16,128]{2,1,0:T(8,128)(2,1)S(1)} %slice.4.up_ref), custom_call_target="tpu_custom_call" | custom-call | tf_op jit(solution)/shard_map/pallas_call | solution.py:187
  36.9 11.9 %all-to-all-start.1 = ((bf16[32,72,128]{2,1,0:T(8,128)(2,1)}), bf16[32,72,128]{2,1,0:T(8,128)(2,1)S(1)}, u32[]{:S(2)}, u32[]{:S(2)}) async-start(bf16[32,72,128]{2,1,0:T(8,128)(2,1)} %bitcast.7), calls=%async_computation.1 | async-start | bytes 1179648 | tf_op jit(solution)/shard_map/all_to_all | solution.py:183
  48.8 0.0 collective-permute-done.1.refs_1_
  48.8 4.9 %collective-permute-start.2 = (bf16[2,224,512]{2,1,0:T(8,128)(2,1)S(1)}, bf16[2,224,512]{2,1,0:T(8,128)(2,1)S(1)}, u32[]{:S(2)}, u32[]{:S(2)}) collective-permute-start(bf16[2,224,512]{2,1,0:T(8,128)(2,1)S(1)} %collective-permute-done.1.refs_1_), channel_id=1, source_target_pairs={{0,2},{1,15},{2,4},{3,1},{4,6},{5,3},{6,8},{7,5},{8,10},{9,7},{10,... | collective-permute-start | bytes 1376264 | tf_op jit(solution)/shard_map/ppermute | solution.py:225
  53.8 5.4 %collective-permute-done.2.refs_2_ = bf16[2,224,512]{2,1,0:T(8,128)(2,1)S(1)} collective-permute-done((bf16[2,224,512]{2,1,0:T(8,128)(2,1)S(1)}, bf16[2,224,512]{2,1,0:T(8,128)(2,1)S(1)}, u32[]{:S(2)}, u32[]{:S(2)}) %collective-permute-start.2) | collective-permute-done | bytes 458784 | tf_op jit(solution)/shard_map/ppermute | solution.py:225
  59.2 5.3 %collective-permute-start.3 = (bf16[2,224,512]{2,1,0:T(8,128)(2,1)S(1)}, bf16[2,224,512]{2,1,0:T(8,128)(2,1)S(1)}, u32[]{:S(2)}, u32[]{:S(2)}) collective-permute-start(bf16[2,224,512]{2,1,0:T(8,128)(2,1)S(1)} %collective-permute-done.2.refs_2_), channel_id=1, source_target_pairs={{0,2},{1,15},{2,4},{3,1},{4,6},{5,3},{6,8},{7,5},{8,10},{9,7},{10,... | collective-permute-start | bytes 1376264 | tf_op jit(solution)/shard_map/ppermute | solution.py:225
  64.5 2.3 %all-to-all-done.1 = bf16[32,72,128]{2,1,0:T(8,128)(2,1)S(1)} async-done(((bf16[32,72,128]{2,1,0:T(8,128)(2,1)}), bf16[32,72,128]{2,1,0:T(8,128)(2,1)S(1)}, u32[]{:S(2)}, u32[]{:S(2)}) %all-to-all-start.1) | async-done | bytes 589856 | tf_op jit(solution)/shard_map/all_to_all | solution.py:183
  66.7 1.2 %shard_map.57 = bf16[32,16,128]{2,1,0:T(8,128)(2,1)} custom-call(bf16[32,9,8,128]{3,2,1,0:T(8,128)(2,1)S(1)} %bitcast.16, bf16[2,512,128]{2,1,0:T(8,128)(2,1)S(1)} %collective-permute-done.up_ref), custom_call_target="tpu_custom_call" | custom-call | tf_op jit(solution)/shard_map/pallas_call | solution.py:187
  67.9 7.0 %all-to-all-start.2 = ((bf16[32,16,128]{2,1,0:T(8,128)(2,1)}), bf16[32,16,128]{2,1,0:T(8,128)(2,1)S(1)}, u32[]{:S(2)}, u32[]{:S(2)}) async-start(bf16[32,16,128]{2,1,0:T(8,128)(2,1)} %shard_map.57), calls=%async_computation.2 | async-start | bytes 262144 | tf_op jit(solution)/shard_map/all_to_all | solution.py:183
  74.9 0.0 collective-permute-done.3.refs_3_
  74.9 3.0 %collective-permute-start.4 = (bf16[224,512]{1,0:T(8,128)(2,1)S(1)}, bf16[224,512]{1,0:T(8,128)(2,1)S(1)}, u32[]{:S(2)}, u32[]{:S(2)}) collective-permute-start(bf16[224,512]{1,0:T(8,128)(2,1)S(1)} %dynamic-slice_bitcast_fusion), channel_id=1, source_target_pairs={{0,2},{1,15},{2,4},{3,1},{4,6},{5,3},{6,8},{7,5},{8,10},{9,7},{10,... | collective-permute-start | bytes 688136 | tf_op jit(solution)/shard_map/ppermute | solution.py:227
  77.9 0.1 pad_add_fusion.place_ref
  78.0 6.0 %all-to-all-done.2 = bf16[32,16,128]{2,1,0:T(8,128)(2,1)S(1)} async-done(((bf16[32,16,128]{2,1,0:T(8,128)(2,1)}), bf16[32,16,128]{2,1,0:T(8,128)(2,1)S(1)}, u32[]{:S(2)}, u32[]{:S(2)}) %all-to-all-start.2) | async-done | bytes 131104 | tf_op jit(solution)/shard_map/all_to_all | solution.py:183
  84.0 3.7 %all-gather = bf16[64,16,128]{2,1,0:T(8,128)(2,1)S(1)} all-gather(bf16[32,16,128]{2,1,0:T(8,128)(2,1)S(1)} %all-to-all-done.2), channel_id=2, replica_groups=mesh['seq'=32,'z'=8,'core'=2] {'core'}, dimensions={0}, use_global_device_ids=true | all-gather | bytes 393216 | tf_op jit(solution)/shard_map/all_gather | solution.py:269
  87.7 0.0 collective-permute-done.4.refs_4_
  87.7 0.0 copy-done.1
  87.7 1.2 %shard_map.58 = f32[2,8,224]{2,1,0:T(8,128)S(1)} custom-call(s32[2]{0:T(128)S(1)} %pad_add_fusion.place_ref, bf16[2,32,16,128]{3,2,1,0:T(8,128)(2,1)S(1)} %bitcast.17, bf16[224,512]{1,0:T(8,128)(2,1)S(1)} %bitcast.19, bf16[2,224,512]{2,1,0:T(8,128)(2,1)S(1)} %collective-permute-done.1.refs_1_, bf16[2,224,512]{2,1,0:T(8,128)(2,1)S(1)} %collective-permute-done.2.refs_2_, ...), custom_call_target="tpu_custom_call" | custom-call | tf_op jit(solution)/shard_map/pallas_call | solution.py:187
  88.9 1.9 %all-gather.2 = f32[4,8,224]{2,1,0:T(8,128)S(1)} all-gather(f32[2,8,224]{2,1,0:T(8,128)S(1)} %shard_map.58), channel_id=4, replica_groups=mesh['seq'=32,'z'=8,'core'=2] {'core'}, dimensions={0}, use_global_device_ids=true | all-gather | bytes 43008 | tf_op jit(solution)/shard_map/all_gather | solution.py:272
  90.7 0.6 convert_element_type.7
  (4 shorter events, 0.1 us)
Async XLA Ops:
  0.0 12.2 %copy-start = (bf16[4,512,128]{2,1,0:T(8,128)(2,1)S(1)}, bf16[4,512,128]{2,1,0:T(8,128)(2,1)}, u32[]{:S(2)}) copy-start(bf16[4,512,128]{2,1,0:T(8,128)(2,1)} %param.8) | copy-start | bytes 1572868
  0.0 0.8 copy-start.2
  1.7 27.5 %all-to-all-start = ((bf16[32,72,128]{2,1,0:T(8,128)(2,1)}), bf16[32,72,128]{2,1,0:T(8,128)(2,1)S(1)}, u32[]{:S(2)}, u32[]{:S(2)}) async-start(bf16[32,72,128]{2,1,0:T(8,128)(2,1)} %bitcast.4), calls=%async_computation | async-start | bytes 1179648 | tf_op jit(solution)/shard_map/all_to_all | solution.py:183
  12.3 16.9 %collective-permute-start = (bf16[2,512,128]{2,1,0:T(8,128)(2,1)S(1)}, bf16[2,512,128]{2,1,0:T(8,128)(2,1)S(1)}, u32[]{:S(2)}, u32[]{:S(2)}) collective-permute-start(bf16[2,512,128]{2,1,0:T(8,128)(2,1)S(1)} %constant_dynamic-slice_fusion), channel_id=1, source_target_pairs={{0,0},{9,1},{6,2},{15,3},{12,4},{5,5},{2,6},{11,7},{8,8},{1,9},{14... | collective-permute-start | bytes 786440 | tf_op jit(solution)/shard_map/ppermute | solution.py:236
  25.3 62.4 %copy-start.1 = (bf16[512,224]{0,1:T(8,128)(2,1)S(1)}, bf16[512,224]{0,1:T(8,128)(2,1)}, u32[]{:S(2)}) copy-start(bf16[512,224]{0,1:T(8,128)(2,1)} %param.9) | copy-start | bytes 688132
  25.3 23.5 %collective-permute-start.1 = (bf16[2,224,512]{2,1,0:T(8,128)(2,1)S(1)}, bf16[2,224,512]{2,1,0:T(8,128)(2,1)S(1)}, u32[]{:S(2)}, u32[]{:S(2)}) collective-permute-start(bf16[2,224,512]{2,1,0:T(8,128)(2,1)S(1)} %bitcast.21), channel_id=1, source_target_pairs={{0,2},{1,15},{2,4},{3,1},{4,6},{5,3},{6,8},{7,5},{8,10},{9,7},{10,... | collective-permute-start | bytes 1376264 | tf_op jit(solution)/shard_map/ppermute | solution.py:225
  36.9 29.9 %all-to-all-start.1 = ((bf16[32,72,128]{2,1,0:T(8,128)(2,1)}), bf16[32,72,128]{2,1,0:T(8,128)(2,1)S(1)}, u32[]{:S(2)}, u32[]{:S(2)}) async-start(bf16[32,72,128]{2,1,0:T(8,128)(2,1)} %bitcast.7), calls=%async_computation.1 | async-start | bytes 1179648 | tf_op jit(solution)/shard_map/all_to_all | solution.py:183
  48.8 10.3 %collective-permute-start.2 = (bf16[2,224,512]{2,1,0:T(8,128)(2,1)S(1)}, bf16[2,224,512]{2,1,0:T(8,128)(2,1)S(1)}, u32[]{:S(2)}, u32[]{:S(2)}) collective-permute-start(bf16[2,224,512]{2,1,0:T(8,128)(2,1)S(1)} %collective-permute-done.1.refs_1_), channel_id=1, source_target_pairs={{0,2},{1,15},{2,4},{3,1},{4,6},{5,3},{6,8},{7,5},{8,10},{9,7},{10,... | collective-permute-start | bytes 1376264 | tf_op jit(solution)/shard_map/ppermute | solution.py:225
  59.2 15.7 %collective-permute-start.3 = (bf16[2,224,512]{2,1,0:T(8,128)(2,1)S(1)}, bf16[2,224,512]{2,1,0:T(8,128)(2,1)S(1)}, u32[]{:S(2)}, u32[]{:S(2)}) collective-permute-start(bf16[2,224,512]{2,1,0:T(8,128)(2,1)S(1)} %collective-permute-done.2.refs_2_), channel_id=1, source_target_pairs={{0,2},{1,15},{2,4},{3,1},{4,6},{5,3},{6,8},{7,5},{8,10},{9,7},{10,... | collective-permute-start | bytes 1376264 | tf_op jit(solution)/shard_map/ppermute | solution.py:225
  67.9 16.1 %all-to-all-start.2 = ((bf16[32,16,128]{2,1,0:T(8,128)(2,1)}), bf16[32,16,128]{2,1,0:T(8,128)(2,1)S(1)}, u32[]{:S(2)}, u32[]{:S(2)}) async-start(bf16[32,16,128]{2,1,0:T(8,128)(2,1)} %shard_map.57), calls=%async_computation.2 | async-start | bytes 262144 | tf_op jit(solution)/shard_map/all_to_all | solution.py:183
  74.9 12.8 %collective-permute-start.4 = (bf16[224,512]{1,0:T(8,128)(2,1)S(1)}, bf16[224,512]{1,0:T(8,128)(2,1)S(1)}, u32[]{:S(2)}, u32[]{:S(2)}) collective-permute-start(bf16[224,512]{1,0:T(8,128)(2,1)S(1)} %dynamic-slice_bitcast_fusion), channel_id=1, source_target_pairs={{0,2},{1,15},{2,4},{3,1},{4,6},{5,3},{6,8},{7,5},{8,10},{9,7},{10,... | collective-permute-start | bytes 688136 | tf_op jit(solution)/shard_map/ppermute | solution.py:227

commit v4 on v3

--- a/solution.py
+++ b/solution.py
@@ -14,7 +14,6 @@
 
 NEG = -1e30
 LANES = 128
-PARTS = 4
 PIECES = 5
 VMEM = pl.BlockSpec(memory_space=pltpu.VMEM)
 HBM = pl.BlockSpec(memory_space=pltpu.HBM)
@@ -67,29 +66,17 @@
     position = lax.broadcasted_iota(jnp.int32, (all_rows, ctx_dev), 1)
     lane = lax.broadcasted_iota(jnp.int32, (all_rows, LANES), 1)
     start, core = scalars_ref[seqs + 1], scalars_ref[seqs + 2]
-    part = ctx_dev // PARTS
-    copies = {}
-    for b in range(seqs):
-        for k in range(PARTS):
-            at = pl.ds(k * part, part)
-            copies[b, k] = pltpu.make_async_copy(
-                cache_ref.at[b, :, at], keys_ref.at[b, :, at], sems.at[b, k]
-            )
-    for k in range(PARTS):
-        copies[0, k].start()
+    copies = [pltpu.make_async_copy(cache_ref.at[b], keys_ref.at[b], sems.at[b]) for b in range(seqs)]
+    copies[0].start()
     extra = jnp.zeros((all_rows, LANES), jnp.float32)
     for b in range(seqs):
         blocks = [q_ref[:, b * whole + c].reshape(all_rows, LANES) for c in range(whole)]
         rest = q_ref[:, seqs * whole].reshape(all_rows, LANES)
         queries = jnp.concatenate(blocks + [rest[:, b * left : (b + 1) * left]], axis=1)
-        scores = []
-        for k in range(PARTS):
-            copies[b, k].wait()
-            if b + 1 < seqs:
-                copies[b + 1, k].start()
-            keys = keys_ref[b, :, k * part : (k + 1) * part]
-            scores.append(jnp.dot(queries, keys, preferred_element_type=jnp.float32))
-        scores = jnp.concatenate(scores, axis=1)
+        copies[b].wait()
+        if b + 1 < seqs:
+            copies[b + 1].start()
+        scores = jnp.dot(queries, keys_ref[b], preferred_element_type=jnp.float32)
         limit = scalars_ref[b] - ahead + 1 - scalars_ref[seqs] + step
         masked = jnp.where(position < limit, scores, NEG)
         top = jnp.max(masked, axis=1, keepdims=True)
@@ -246,7 +233,7 @@
         up[:, :16],
         scratch=[
             pltpu.VMEM((seqs, width, ctx_dev), bf16),
-            pltpu.SemaphoreType.DMA((seqs, PARTS)),
+            pltpu.SemaphoreType.DMA((seqs,)),
         ],
         limit=52,
     )

time: 91.9 us -> 91.4 us (level)
  transfers between devices with their start and end apart: 8 -> 8, of which waited for: 3 -> 3; matrix products, arithmetic and copies ran while one was open for 1% -> 1% of each run, Pallas kernels for 10% -> 9%
where the time goes in v4:
time: 91.4 us; the launch traced here: 90.9 us
  starting transfers between devices  56.4 us (62%)
  waiting for transfers between devices  13.7 us (15%)
  Pallas kernels  10.4 us (11%)
  blocking collectives  7.89 us (9%)
  local copies, waits for them, and re-layouts  1.45 us (2%)
    all_to_all x3, starting transfers between devices, exchange(): return lax.all_to_all(flat, 'seq', 0, 0, tiled=True).reshape(blocks.shape)  29.4 us
    ppermute x3, starting transfers between devices, per_device(): block = lax.ppermute(block, batch, ring)  13.4 us
    ppermute x1, starting transfers between devices, per_device(): up = lax.ppermute(mine, ('seq', 'z', 'core'), pairs)  10.6 us
    pallas_call x4, Pallas kernels, call(): pl.pallas_call(kernel, out_shape=jax.ShapeDtypeStruct(shape, dtype), in_s...  10.4 us
    all_to_all x3, waiting for transfers between devices, exchange(): return lax.all_to_all(flat, 'seq', 0, 0, tiled=True).reshape(blocks.shape)  8.32 us
    ppermute x3, waiting for transfers between devices, per_device(): block = lax.ppermute(block, batch, ring)  5.41 us
    all_gather x1, blocking collectives, per_device(): lax.all_gather(values, 'core')  3.68 us
    ppermute x1, starting transfers between devices, per_device(): lax.ppermute(lax.dynamic_index_in_dim(block, core, 0, False), batch, ring)  2.98 us
  transfers between devices with their start and end apart: 8, of which 3 were waited for; matrix products, arithmetic and copies ran while one was open for 1% of the time, Pallas kernels for 9%

profile of v4, /device:TPU:1, one launch (start us, length us, event | category | flops | bytes accessed | tf_op | source)
XLA Modules:
  0.0 90.9 jit_solution(7970723629749252958)
XLA Ops:
  0.0 0.0 copy-start
  0.0 0.0 copy-start.2
  0.0 0.8 copy-done.2
  0.8 0.9 %shard_map.55 = bf16[32,9,8,128]{3,2,1,0:T(8,128)(2,1)} custom-call(bf16[2,4,2,576]{3,2,1,0:T(2,128)(2,1)S(1)} %copy-done.2), custom_call_target="tpu_custom_call" | custom-call | tf_op jit(solution)/shard_map/pallas_call | solution.py:174
  1.7 10.5 %all-to-all-start = ((bf16[32,72,128]{2,1,0:T(8,128)(2,1)}), bf16[32,72,128]{2,1,0:T(8,128)(2,1)S(1)}, u32[]{:S(2)}, u32[]{:S(2)}) async-start(bf16[32,72,128]{2,1,0:T(8,128)(2,1)} %bitcast.4), calls=%async_computation | async-start | bytes 1179648 | tf_op jit(solution)/shard_map/all_to_all | solution.py:170
  12.2 0.0 copy-done
  12.3 10.6 %collective-permute-start = (bf16[2,512,128]{2,1,0:T(8,128)(2,1)S(1)}, bf16[2,512,128]{2,1,0:T(8,128)(2,1)S(1)}, u32[]{:S(2)}, u32[]{:S(2)}) collective-permute-start(bf16[2,512,128]{2,1,0:T(8,128)(2,1)S(1)} %constant_dynamic-slice_fusion), channel_id=1, source_target_pairs={{0,0},{9,1},{6,2},{15,3},{12,4},{5,5},{2,6},{11,7},{8,8},{1,9},{14... | collective-permute-start | bytes 786440 | tf_op jit(solution)/shard_map/ppermute | solution.py:223
  22.9 2.3 %all-gather.1 = bf16[448,512]{1,0:T(8,128)(2,1)S(1)} all-gather(bf16[224,512]{1,0:T(8,128)(2,1)} %bitcast.18), channel_id=3, replica_groups=mesh['seq'=32,'z'=8,'core'=2] {'core'}, dimensions={0}, use_global_device_ids=true | all-gather | bytes 688128 | tf_op jit(solution)/shard_map/all_gather | solution.py:209
  25.3 0.0 copy-start.1
  25.3 3.2 %collective-permute-start.1 = (bf16[2,224,512]{2,1,0:T(8,128)(2,1)S(1)}, bf16[2,224,512]{2,1,0:T(8,128)(2,1)S(1)}, u32[]{:S(2)}, u32[]{:S(2)}) collective-permute-start(bf16[2,224,512]{2,1,0:T(8,128)(2,1)S(1)} %bitcast.21), channel_id=1, source_target_pairs={{0,2},{1,15},{2,4},{3,1},{4,6},{5,3},{6,8},{7,5},{8,10},{9,7},{10,... | collective-permute-start | bytes 1376264 | tf_op jit(solution)/shard_map/ppermute | solution.py:212
  28.5 0.7 pad_add_fusion.1.scalars_ref
  29.2 0.0 collective-permute-done.up_ref
  29.2 0.0 all-to-all-done
  29.2 7.2 %shard_map.56 = bf16[32,9,8,128]{3,2,1,0:T(8,128)(2,1)} custom-call(s32[5]{0:T(128)S(1)} %pad_add_fusion.1.scalars_ref, bf16[32,9,8,128]{3,2,1,0:T(8,128)(2,1)S(1)} %bitcast.15, bf16[2,576,2048]{2,1,0:T(8,128)(2,1)} %bitcast.20, bf16[2,16,128]{2,1,0:T(8,128)(2,1)S(1)} %slice.4.up_ref), custom_call_target="tpu_custom_call" | custom-call | tf_op jit(solution)/shard_map/pallas_call | solution.py:174
  36.4 11.9 %all-to-all-start.1 = ((bf16[32,72,128]{2,1,0:T(8,128)(2,1)}), bf16[32,72,128]{2,1,0:T(8,128)(2,1)S(1)}, u32[]{:S(2)}, u32[]{:S(2)}) async-start(bf16[32,72,128]{2,1,0:T(8,128)(2,1)} %bitcast.7), calls=%async_computation.1 | async-start | bytes 1179648 | tf_op jit(solution)/shard_map/all_to_all | solution.py:170
  48.3 0.0 collective-permute-done.1.refs_1_
  48.3 4.9 %collective-permute-start.2 = (bf16[2,224,512]{2,1,0:T(8,128)(2,1)S(1)}, bf16[2,224,512]{2,1,0:T(8,128)(2,1)S(1)}, u32[]{:S(2)}, u32[]{:S(2)}) collective-permute-start(bf16[2,224,512]{2,1,0:T(8,128)(2,1)S(1)} %collective-permute-done.1.refs_1_), channel_id=1, source_target_pairs={{0,2},{1,15},{2,4},{3,1},{4,6},{5,3},{6,8},{7,5},{8,10},{9,7},{10,... | collective-permute-start | bytes 1376264 | tf_op jit(solution)/shard_map/ppermute | solution.py:212
  53.3 5.4 %collective-permute-done.2.refs_2_ = bf16[2,224,512]{2,1,0:T(8,128)(2,1)S(1)} collective-permute-done((bf16[2,224,512]{2,1,0:T(8,128)(2,1)S(1)}, bf16[2,224,512]{2,1,0:T(8,128)(2,1)S(1)}, u32[]{:S(2)}, u32[]{:S(2)}) %collective-permute-start.2) | collective-permute-done | bytes 458784 | tf_op jit(solution)/shard_map/ppermute | solution.py:212
  58.7 5.3 %collective-permute-start.3 = (bf16[2,224,512]{2,1,0:T(8,128)(2,1)S(1)}, bf16[2,224,512]{2,1,0:T(8,128)(2,1)S(1)}, u32[]{:S(2)}, u32[]{:S(2)}) collective-permute-start(bf16[2,224,512]{2,1,0:T(8,128)(2,1)S(1)} %collective-permute-done.2.refs_2_), channel_id=1, source_target_pairs={{0,2},{1,15},{2,4},{3,1},{4,6},{5,3},{6,8},{7,5},{8,10},{9,7},{10,... | collective-permute-start | bytes 1376264 | tf_op jit(solution)/shard_map/ppermute | solution.py:212
  64.0 2.3 %all-to-all-done.1 = bf16[32,72,128]{2,1,0:T(8,128)(2,1)S(1)} async-done(((bf16[32,72,128]{2,1,0:T(8,128)(2,1)}), bf16[32,72,128]{2,1,0:T(8,128)(2,1)S(1)}, u32[]{:S(2)}, u32[]{:S(2)}) %all-to-all-start.1) | async-done | bytes 589856 | tf_op jit(solution)/shard_map/all_to_all | solution.py:170
  66.2 1.2 %shard_map.57 = bf16[32,16,128]{2,1,0:T(8,128)(2,1)} custom-call(bf16[32,9,8,128]{3,2,1,0:T(8,128)(2,1)S(1)} %bitcast.16, bf16[2,512,128]{2,1,0:T(8,128)(2,1)S(1)} %collective-permute-done.up_ref), custom_call_target="tpu_custom_call" | custom-call | tf_op jit(solution)/shard_map/pallas_call | solution.py:174
  67.4 7.0 %all-to-all-start.2 = ((bf16[32,16,128]{2,1,0:T(8,128)(2,1)}), bf16[32,16,128]{2,1,0:T(8,128)(2,1)S(1)}, u32[]{:S(2)}, u32[]{:S(2)}) async-start(bf16[32,16,128]{2,1,0:T(8,128)(2,1)} %shard_map.57), calls=%async_computation.2 | async-start | bytes 262144 | tf_op jit(solution)/shard_map/all_to_all | solution.py:170
  74.4 0.0 collective-permute-done.3.refs_3_
  74.4 3.0 %collective-permute-start.4 = (bf16[224,512]{1,0:T(8,128)(2,1)S(1)}, bf16[224,512]{1,0:T(8,128)(2,1)S(1)}, u32[]{:S(2)}, u32[]{:S(2)}) collective-permute-start(bf16[224,512]{1,0:T(8,128)(2,1)S(1)} %dynamic-slice_bitcast_fusion), channel_id=1, source_target_pairs={{0,2},{1,15},{2,4},{3,1},{4,6},{5,3},{6,8},{7,5},{8,10},{9,7},{10,... | collective-permute-start | bytes 688136 | tf_op jit(solution)/shard_map/ppermute | solution.py:214
  77.4 0.1 pad_add_fusion.place_ref
  77.5 6.0 %all-to-all-done.2 = bf16[32,16,128]{2,1,0:T(8,128)(2,1)S(1)} async-done(((bf16[32,16,128]{2,1,0:T(8,128)(2,1)}), bf16[32,16,128]{2,1,0:T(8,128)(2,1)S(1)}, u32[]{:S(2)}, u32[]{:S(2)}) %all-to-all-start.2) | async-done | bytes 131104 | tf_op jit(solution)/shard_map/all_to_all | solution.py:170
  83.5 3.7 %all-gather = bf16[64,16,128]{2,1,0:T(8,128)(2,1)S(1)} all-gather(bf16[32,16,128]{2,1,0:T(8,128)(2,1)S(1)} %all-to-all-done.2), channel_id=2, replica_groups=mesh['seq'=32,'z'=8,'core'=2] {'core'}, dimensions={0}, use_global_device_ids=true | all-gather | bytes 393216 | tf_op jit(solution)/shard_map/all_gather | solution.py:256
  87.2 0.0 collective-permute-done.4.refs_4_
  87.2 0.0 copy-done.1
  87.2 1.2 %shard_map.58 = f32[2,8,224]{2,1,0:T(8,128)S(1)} custom-call(s32[2]{0:T(128)S(1)} %pad_add_fusion.place_ref, bf16[2,32,16,128]{3,2,1,0:T(8,128)(2,1)S(1)} %bitcast.17, bf16[224,512]{1,0:T(8,128)(2,1)S(1)} %bitcast.19, bf16[2,224,512]{2,1,0:T(8,128)(2,1)S(1)} %collective-permute-done.1.refs_1_, bf16[2,224,512]{2,1,0:T(8,128)(2,1)S(1)} %collective-permute-done.2.refs_2_, ...), custom_call_target="tpu_custom_call" | custom-call | tf_op jit(solution)/shard_map/pallas_call | solution.py:174
  88.4 1.9 %all-gather.2 = f32[4,8,224]{2,1,0:T(8,128)S(1)} all-gather(f32[2,8,224]{2,1,0:T(8,128)S(1)} %shard_map.58), channel_id=4, replica_groups=mesh['seq'=32,'z'=8,'core'=2] {'core'}, dimensions={0}, use_global_device_ids=true | all-gather | bytes 43008 | tf_op jit(solution)/shard_map/all_gather | solution.py:259
  90.3 0.6 convert_element_type.7
  (4 shorter events, 0.1 us)
Async XLA Ops:
  0.0 12.2 %copy-start = (bf16[4,512,128]{2,1,0:T(8,128)(2,1)S(1)}, bf16[4,512,128]{2,1,0:T(8,128)(2,1)}, u32[]{:S(2)}) copy-start(bf16[4,512,128]{2,1,0:T(8,128)(2,1)} %param.8) | copy-start | bytes 1572868
  0.0 0.8 copy-start.2
  1.7 27.5 %all-to-all-start = ((bf16[32,72,128]{2,1,0:T(8,128)(2,1)}), bf16[32,72,128]{2,1,0:T(8,128)(2,1)S(1)}, u32[]{:S(2)}, u32[]{:S(2)}) async-start(bf16[32,72,128]{2,1,0:T(8,128)(2,1)} %bitcast.4), calls=%async_computation | async-start | bytes 1179648 | tf_op jit(solution)/shard_map/all_to_all | solution.py:170
  12.3 16.9 %collective-permute-start = (bf16[2,512,128]{2,1,0:T(8,128)(2,1)S(1)}, bf16[2,512,128]{2,1,0:T(8,128)(2,1)S(1)}, u32[]{:S(2)}, u32[]{:S(2)}) collective-permute-start(bf16[2,512,128]{2,1,0:T(8,128)(2,1)S(1)} %constant_dynamic-slice_fusion), channel_id=1, source_target_pairs={{0,0},{9,1},{6,2},{15,3},{12,4},{5,5},{2,6},{11,7},{8,8},{1,9},{14... | collective-permute-start | bytes 786440 | tf_op jit(solution)/shard_map/ppermute | solution.py:223
  25.3 61.9 %copy-start.1 = (bf16[512,224]{0,1:T(8,128)(2,1)S(1)}, bf16[512,224]{0,1:T(8,128)(2,1)}, u32[]{:S(2)}) copy-start(bf16[512,224]{0,1:T(8,128)(2,1)} %param.9) | copy-start | bytes 688132
  25.3 23.1 %collective-permute-start.1 = (bf16[2,224,512]{2,1,0:T(8,128)(2,1)S(1)}, bf16[2,224,512]{2,1,0:T(8,128)(2,1)S(1)}, u32[]{:S(2)}, u32[]{:S(2)}) collective-permute-start(bf16[2,224,512]{2,1,0:T(8,128)(2,1)S(1)} %bitcast.21), channel_id=1, source_target_pairs={{0,2},{1,15},{2,4},{3,1},{4,6},{5,3},{6,8},{7,5},{8,10},{9,7},{10,... | collective-permute-start | bytes 1376264 | tf_op jit(solution)/shard_map/ppermute | solution.py:212
  36.4 29.9 %all-to-all-start.1 = ((bf16[32,72,128]{2,1,0:T(8,128)(2,1)}), bf16[32,72,128]{2,1,0:T(8,128)(2,1)S(1)}, u32[]{:S(2)}, u32[]{:S(2)}) async-start(bf16[32,72,128]{2,1,0:T(8,128)(2,1)} %bitcast.7), calls=%async_computation.1 | async-start | bytes 1179648 | tf_op jit(solution)/shard_map/all_to_all | solution.py:170
  48.3 10.3 %collective-permute-start.2 = (bf16[2,224,512]{2,1,0:T(8,128)(2,1)S(1)}, bf16[2,224,512]{2,1,0:T(8,128)(2,1)S(1)}, u32[]{:S(2)}, u32[]{:S(2)}) collective-permute-start(bf16[2,224,512]{2,1,0:T(8,128)(2,1)S(1)} %collective-permute-done.1.refs_1_), channel_id=1, source_target_pairs={{0,2},{1,15},{2,4},{3,1},{4,6},{5,3},{6,8},{7,5},{8,10},{9,7},{10,... | collective-permute-start | bytes 1376264 | tf_op jit(solution)/shard_map/ppermute | solution.py:212
  58.7 15.7 %collective-permute-start.3 = (bf16[2,224,512]{2,1,0:T(8,128)(2,1)S(1)}, bf16[2,224,512]{2,1,0:T(8,128)(2,1)S(1)}, u32[]{:S(2)}, u32[]{:S(2)}) collective-permute-start(bf16[2,224,512]{2,1,0:T(8,128)(2,1)S(1)} %collective-permute-done.2.refs_2_), channel_id=1, source_target_pairs={{0,2},{1,15},{2,4},{3,1},{4,6},{5,3},{6,8},{7,5},{8,10},{9,7},{10,... | collective-permute-start | bytes 1376264 | tf_op jit(solution)/shard_map/ppermute | solution.py:212
  67.4 16.1 %all-to-all-start.2 = ((bf16[32,16,128]{2,1,0:T(8,128)(2,1)}), bf16[32,16,128]{2,1,0:T(8,128)(2,1)S(1)}, u32[]{:S(2)}, u32[]{:S(2)}) async-start(bf16[32,16,128]{2,1,0:T(8,128)(2,1)} %shard_map.57), calls=%async_computation.2 | async-start | bytes 262144 | tf_op jit(solution)/shard_map/all_to_all | solution.py:170
  74.4 12.8 %collective-permute-start.4 = (bf16[224,512]{1,0:T(8,128)(2,1)S(1)}, bf16[224,512]{1,0:T(8,128)(2,1)S(1)}, u32[]{:S(2)}, u32[]{:S(2)}) collective-permute-start(bf16[224,512]{1,0:T(8,128)(2,1)S(1)} %dynamic-slice_bitcast_fusion), channel_id=1, source_target_pairs={{0,2},{1,15},{2,4},{3,1},{4,6},{5,3},{6,8},{7,5},{8,10},{9,7},{10,... | collective-permute-start | bytes 688136 | tf_op jit(solution)/shard_map/ppermute | solution.py:214

commit v5 on v4

--- a/solution.py
+++ b/solution.py
@@ -15,6 +15,7 @@
 NEG = -1e30
 LANES = 128
 PIECES = 5
+PARTS = 4
 VMEM = pl.BlockSpec(memory_space=pltpu.VMEM)
 HBM = pl.BlockSpec(memory_space=pltpu.HBM)
 SMEM = pl.BlockSpec(memory_space=pltpu.SMEM)
@@ -63,31 +64,47 @@
     base2 = scale * 1.4426950408889634
     row = lax.broadcasted_iota(jnp.int32, (all_rows, 1), 0)
     step = lax.rem(row, ahead)
-    position = lax.broadcasted_iota(jnp.int32, (all_rows, ctx_dev), 1)
     lane = lax.broadcasted_iota(jnp.int32, (all_rows, LANES), 1)
     start, core = scalars_ref[seqs + 1], scalars_ref[seqs + 2]
     copies = [pltpu.make_async_copy(cache_ref.at[b], keys_ref.at[b], sems.at[b]) for b in range(seqs)]
-    copies[0].start()
+    for copy in copies:
+        copy.start()
+    part = ctx_dev // PARTS
+    rest = q_ref[:, seqs * whole].reshape(all_rows, LANES)
+
+    def masked_scores(b, k):
+        blocks = [q_ref[:, b * whole + c].reshape(all_rows, LANES) for c in range(whole)]
+        queries = jnp.concatenate(blocks + [rest[:, b * left : (b + 1) * left]], axis=1)
+        keys = keys_ref[b, :, k * part : (k + 1) * part]
+        scores = jnp.dot(queries, keys, preferred_element_type=jnp.float32)
+        limit = scalars_ref[b] - ahead + 1 - scalars_ref[seqs] + step
+        position = lax.broadcasted_iota(jnp.int32, (all_rows, part), 1) + k * part
+        return jnp.where(position < limit, scores, NEG)
+
     extra = jnp.zeros((all_rows, LANES), jnp.float32)
+    copies[0].wait()
+    scores = [masked_scores(0, k) for k in range(PARTS)]
     for b in range(seqs):
-        blocks = [q_ref[:, b * whole + c].reshape(all_rows, LANES) for c in range(whole)]
-        rest = q_ref[:, seqs * whole].reshape(all_rows, LANES)
-        queries = jnp.concatenate(blocks + [rest[:, b * left : (b + 1) * left]], axis=1)
-        copies[b].wait()
         if b + 1 < seqs:
-            copies[b + 1].start()
-        scores = jnp.dot(queries, keys_ref[b], preferred_element_type=jnp.float32)
-        limit = scalars_ref[b] - ahead + 1 - scalars_ref[seqs] + step
-        masked = jnp.where(position < limit, scores, NEG)
-        top = jnp.max(masked, axis=1, keepdims=True)
-        weights = jnp.exp2((masked - jnp.maximum(top, 0.1 * NEG)) * base2)
-        total = jnp.sum(weights, axis=1, keepdims=True)
-        out = lax.dot_general(
-            weights.astype(jnp.bfloat16),
-            keys_ref[b, :latent],
-            (((1,), (1,)), ((), ())),
-            preferred_element_type=jnp.float32,
-        )
+            copies[b + 1].wait()
+        top = jnp.max(scores[0], axis=1, keepdims=True)
+        for one in scores[1:]:
+            top = jnp.maximum(top, jnp.max(one, axis=1, keepdims=True))
+        total = jnp.zeros((all_rows, 1), jnp.float32)
+        out = jnp.zeros((all_rows, latent), jnp.float32)
+        following = []
+        for k in range(PARTS):
+            weights = jnp.exp2((scores[k] - jnp.maximum(top, 0.1 * NEG)) * base2)
+            total += jnp.sum(weights, axis=1, keepdims=True)
+            out += lax.dot_general(
+                weights.astype(jnp.bfloat16),
+                keys_ref[b, :latent, k * part : (k + 1) * part],
+                (((1,), (1,)), ((), ())),
+                preferred_element_type=jnp.float32,
+            )
+            if b + 1 < seqs:
+                following.append(masked_scores(b + 1, k))
+        scores = following
         for at, piece in enumerate(split(top * scale, 3) + split(total, 2)):
             extra = jnp.where(lane == PIECES * b + at, piece, extra)
         out = out.astype(jnp.bfloat16)

time: 91.4 us -> 90.8 us (level)
  no operation moved by 1% of the time
where the time goes in v5:
time: 90.8 us; the launch traced here: 90.3 us
  starting transfers between devices  56.4 us (62%)
  waiting for transfers between devices  13.7 us (15%)
  Pallas kernels  9.81 us (11%)
  blocking collectives  7.89 us (9%)
  local copies, waits for them, and re-layouts  1.45 us (2%)
    all_to_all x3, starting transfers between devices, exchange(): return lax.all_to_all(flat, 'seq', 0, 0, tiled=True).reshape(blocks.shape)  29.4 us
    ppermute x3, starting transfers between devices, per_device(): block = lax.ppermute(block, batch, ring)  13.4 us
    ppermute x1, starting transfers between devices, per_device(): up = lax.ppermute(mine, ('seq', 'z', 'core'), pairs)  10.6 us
    pallas_call x4, Pallas kernels, call(): pl.pallas_call(kernel, out_shape=jax.ShapeDtypeStruct(shape, dtype), in_s...  9.81 us
    all_to_all x3, waiting for transfers between devices, exchange(): return lax.all_to_all(flat, 'seq', 0, 0, tiled=True).reshape(blocks.shape)  8.32 us
    ppermute x3, waiting for transfers between devices, per_device(): block = lax.ppermute(block, batch, ring)  5.41 us
    all_gather x1, blocking collectives, per_device(): lax.all_gather(values, 'core')  3.68 us
    ppermute x1, starting transfers between devices, per_device(): lax.ppermute(lax.dynamic_index_in_dim(block, core, 0, False), batch, ring)  2.98 us
  transfers between devices with their start and end apart: 8, of which 3 were waited for; matrix products, arithmetic and copies ran while one was open for 1% of the time, Pallas kernels for 9%

profile of v5, /device:TPU:1, one launch (start us, length us, event | category | flops | bytes accessed | tf_op | source)
XLA Modules:
  0.0 90.3 jit_solution(13988853931106813447)
XLA Ops:
  0.0 0.0 copy-start
  0.0 0.0 copy-start.2
  0.0 0.8 copy-done.2
  0.8 0.9 %shard_map.55 = bf16[32,9,8,128]{3,2,1,0:T(8,128)(2,1)} custom-call(bf16[2,4,2,576]{3,2,1,0:T(2,128)(2,1)S(1)} %copy-done.2), custom_call_target="tpu_custom_call" | custom-call | tf_op jit(solution)/shard_map/pallas_call | solution.py:191
  1.7 10.5 %all-to-all-start = ((bf16[32,72,128]{2,1,0:T(8,128)(2,1)}), bf16[32,72,128]{2,1,0:T(8,128)(2,1)S(1)}, u32[]{:S(2)}, u32[]{:S(2)}) async-start(bf16[32,72,128]{2,1,0:T(8,128)(2,1)} %bitcast.4), calls=%async_computation | async-start | bytes 1179648 | tf_op jit(solution)/shard_map/all_to_all | solution.py:187
  12.2 0.0 copy-done
  12.3 10.6 %collective-permute-start = (bf16[2,512,128]{2,1,0:T(8,128)(2,1)S(1)}, bf16[2,512,128]{2,1,0:T(8,128)(2,1)S(1)}, u32[]{:S(2)}, u32[]{:S(2)}) collective-permute-start(bf16[2,512,128]{2,1,0:T(8,128)(2,1)S(1)} %constant_dynamic-slice_fusion), channel_id=1, source_target_pairs={{0,0},{9,1},{6,2},{15,3},{12,4},{5,5},{2,6},{11,7},{8,8},{1,9},{14... | collective-permute-start | bytes 786440 | tf_op jit(solution)/shard_map/ppermute | solution.py:240
  22.9 2.3 %all-gather.1 = bf16[448,512]{1,0:T(8,128)(2,1)S(1)} all-gather(bf16[224,512]{1,0:T(8,128)(2,1)} %bitcast.18), channel_id=3, replica_groups=mesh['seq'=32,'z'=8,'core'=2] {'core'}, dimensions={0}, use_global_device_ids=true | all-gather | bytes 688128 | tf_op jit(solution)/shard_map/all_gather | solution.py:226
  25.3 0.0 copy-start.1
  25.3 3.2 %collective-permute-start.1 = (bf16[2,224,512]{2,1,0:T(8,128)(2,1)S(1)}, bf16[2,224,512]{2,1,0:T(8,128)(2,1)S(1)}, u32[]{:S(2)}, u32[]{:S(2)}) collective-permute-start(bf16[2,224,512]{2,1,0:T(8,128)(2,1)S(1)} %bitcast.21), channel_id=1, source_target_pairs={{0,2},{1,15},{2,4},{3,1},{4,6},{5,3},{6,8},{7,5},{8,10},{9,7},{10,... | collective-permute-start | bytes 1376264 | tf_op jit(solution)/shard_map/ppermute | solution.py:229
  28.5 0.7 pad_add_fusion.1.scalars_ref
  29.2 0.0 collective-permute-done.up_ref
  29.2 0.0 all-to-all-done
  29.2 6.5 %shard_map.56 = bf16[32,9,8,128]{3,2,1,0:T(8,128)(2,1)} custom-call(s32[5]{0:T(128)S(1)} %pad_add_fusion.1.scalars_ref, bf16[32,9,8,128]{3,2,1,0:T(8,128)(2,1)S(1)} %bitcast.15, bf16[2,576,2048]{2,1,0:T(8,128)(2,1)} %bitcast.20, bf16[2,16,128]{2,1,0:T(8,128)(2,1)S(1)} %slice.4.up_ref), custom_call_target="tpu_custom_call" | custom-call | tf_op jit(solution)/shard_map/pallas_call | solution.py:191
  35.8 11.9 %all-to-all-start.1 = ((bf16[32,72,128]{2,1,0:T(8,128)(2,1)}), bf16[32,72,128]{2,1,0:T(8,128)(2,1)S(1)}, u32[]{:S(2)}, u32[]{:S(2)}) async-start(bf16[32,72,128]{2,1,0:T(8,128)(2,1)} %bitcast.7), calls=%async_computation.1 | async-start | bytes 1179648 | tf_op jit(solution)/shard_map/all_to_all | solution.py:187
  47.7 0.0 collective-permute-done.1.refs_1_
  47.7 4.9 %collective-permute-start.2 = (bf16[2,224,512]{2,1,0:T(8,128)(2,1)S(1)}, bf16[2,224,512]{2,1,0:T(8,128)(2,1)S(1)}, u32[]{:S(2)}, u32[]{:S(2)}) collective-permute-start(bf16[2,224,512]{2,1,0:T(8,128)(2,1)S(1)} %collective-permute-done.1.refs_1_), channel_id=1, source_target_pairs={{0,2},{1,15},{2,4},{3,1},{4,6},{5,3},{6,8},{7,5},{8,10},{9,7},{10,... | collective-permute-start | bytes 1376264 | tf_op jit(solution)/shard_map/ppermute | solution.py:229
  52.6 5.4 %collective-permute-done.2.refs_2_ = bf16[2,224,512]{2,1,0:T(8,128)(2,1)S(1)} collective-permute-done((bf16[2,224,512]{2,1,0:T(8,128)(2,1)S(1)}, bf16[2,224,512]{2,1,0:T(8,128)(2,1)S(1)}, u32[]{:S(2)}, u32[]{:S(2)}) %collective-permute-start.2) | collective-permute-done | bytes 458784 | tf_op jit(solution)/shard_map/ppermute | solution.py:229
  58.0 5.3 %collective-permute-start.3 = (bf16[2,224,512]{2,1,0:T(8,128)(2,1)S(1)}, bf16[2,224,512]{2,1,0:T(8,128)(2,1)S(1)}, u32[]{:S(2)}, u32[]{:S(2)}) collective-permute-start(bf16[2,224,512]{2,1,0:T(8,128)(2,1)S(1)} %collective-permute-done.2.refs_2_), channel_id=1, source_target_pairs={{0,2},{1,15},{2,4},{3,1},{4,6},{5,3},{6,8},{7,5},{8,10},{9,7},{10,... | collective-permute-start | bytes 1376264 | tf_op jit(solution)/shard_map/ppermute | solution.py:229
  63.4 2.3 %all-to-all-done.1 = bf16[32,72,128]{2,1,0:T(8,128)(2,1)S(1)} async-done(((bf16[32,72,128]{2,1,0:T(8,128)(2,1)}), bf16[32,72,128]{2,1,0:T(8,128)(2,1)S(1)}, u32[]{:S(2)}, u32[]{:S(2)}) %all-to-all-start.1) | async-done | bytes 589856 | tf_op jit(solution)/shard_map/all_to_all | solution.py:187
  65.6 1.2 %shard_map.57 = bf16[32,16,128]{2,1,0:T(8,128)(2,1)} custom-call(bf16[32,9,8,128]{3,2,1,0:T(8,128)(2,1)S(1)} %bitcast.16, bf16[2,512,128]{2,1,0:T(8,128)(2,1)S(1)} %collective-permute-done.up_ref), custom_call_target="tpu_custom_call" | custom-call | tf_op jit(solution)/shard_map/pallas_call | solution.py:191
  66.8 7.0 %all-to-all-start.2 = ((bf16[32,16,128]{2,1,0:T(8,128)(2,1)}), bf16[32,16,128]{2,1,0:T(8,128)(2,1)S(1)}, u32[]{:S(2)}, u32[]{:S(2)}) async-start(bf16[32,16,128]{2,1,0:T(8,128)(2,1)} %shard_map.57), calls=%async_computation.2 | async-start | bytes 262144 | tf_op jit(solution)/shard_map/all_to_all | solution.py:187
  73.8 0.0 collective-permute-done.3.refs_3_
  73.8 3.0 %collective-permute-start.4 = (bf16[224,512]{1,0:T(8,128)(2,1)S(1)}, bf16[224,512]{1,0:T(8,128)(2,1)S(1)}, u32[]{:S(2)}, u32[]{:S(2)}) collective-permute-start(bf16[224,512]{1,0:T(8,128)(2,1)S(1)} %dynamic-slice_bitcast_fusion), channel_id=1, source_target_pairs={{0,2},{1,15},{2,4},{3,1},{4,6},{5,3},{6,8},{7,5},{8,10},{9,7},{10,... | collective-permute-start | bytes 688136 | tf_op jit(solution)/shard_map/ppermute | solution.py:231
  76.8 0.1 pad_add_fusion.place_ref
  76.9 6.0 %all-to-all-done.2 = bf16[32,16,128]{2,1,0:T(8,128)(2,1)S(1)} async-done(((bf16[32,16,128]{2,1,0:T(8,128)(2,1)}), bf16[32,16,128]{2,1,0:T(8,128)(2,1)S(1)}, u32[]{:S(2)}, u32[]{:S(2)}) %all-to-all-start.2) | async-done | bytes 131104 | tf_op jit(solution)/shard_map/all_to_all | solution.py:187
  82.9 3.7 %all-gather = bf16[64,16,128]{2,1,0:T(8,128)(2,1)S(1)} all-gather(bf16[32,16,128]{2,1,0:T(8,128)(2,1)S(1)} %all-to-all-done.2), channel_id=2, replica_groups=mesh['seq'=32,'z'=8,'core'=2] {'core'}, dimensions={0}, use_global_device_ids=true | all-gather | bytes 393216 | tf_op jit(solution)/shard_map/all_gather | solution.py:273
  86.6 0.0 collective-permute-done.4.refs_4_
  86.6 0.0 copy-done.1
  86.6 1.2 %shard_map.58 = f32[2,8,224]{2,1,0:T(8,128)S(1)} custom-call(s32[2]{0:T(128)S(1)} %pad_add_fusion.place_ref, bf16[2,32,16,128]{3,2,1,0:T(8,128)(2,1)S(1)} %bitcast.17, bf16[224,512]{1,0:T(8,128)(2,1)S(1)} %bitcast.19, bf16[2,224,512]{2,1,0:T(8,128)(2,1)S(1)} %collective-permute-done.1.refs_1_, bf16[2,224,512]{2,1,0:T(8,128)(2,1)S(1)} %collective-permute-done.2.refs_2_, ...), custom_call_target="tpu_custom_call" | custom-call | tf_op jit(solution)/shard_map/pallas_call | solution.py:191
  87.8 1.9 %all-gather.2 = f32[4,8,224]{2,1,0:T(8,128)S(1)} all-gather(f32[2,8,224]{2,1,0:T(8,128)S(1)} %shard_map.58), channel_id=4, replica_groups=mesh['seq'=32,'z'=8,'core'=2] {'core'}, dimensions={0}, use_global_device_ids=true | all-gather | bytes 43008 | tf_op jit(solution)/shard_map/all_gather | solution.py:276
  89.7 0.6 convert_element_type.7
  (4 shorter events, 0.1 us)
Async XLA Ops:
  0.0 12.2 %copy-start = (bf16[4,512,128]{2,1,0:T(8,128)(2,1)S(1)}, bf16[4,512,128]{2,1,0:T(8,128)(2,1)}, u32[]{:S(2)}) copy-start(bf16[4,512,128]{2,1,0:T(8,128)(2,1)} %param.8) | copy-start | bytes 1572868
  0.0 0.8 copy-start.2
  1.7 27.5 %all-to-all-start = ((bf16[32,72,128]{2,1,0:T(8,128)(2,1)}), bf16[32,72,128]{2,1,0:T(8,128)(2,1)S(1)}, u32[]{:S(2)}, u32[]{:S(2)}) async-start(bf16[32,72,128]{2,1,0:T(8,128)(2,1)} %bitcast.4), calls=%async_computation | async-start | bytes 1179648 | tf_op jit(solution)/shard_map/all_to_all | solution.py:187
  12.3 16.9 %collective-permute-start = (bf16[2,512,128]{2,1,0:T(8,128)(2,1)S(1)}, bf16[2,512,128]{2,1,0:T(8,128)(2,1)S(1)}, u32[]{:S(2)}, u32[]{:S(2)}) collective-permute-start(bf16[2,512,128]{2,1,0:T(8,128)(2,1)S(1)} %constant_dynamic-slice_fusion), channel_id=1, source_target_pairs={{0,0},{9,1},{6,2},{15,3},{12,4},{5,5},{2,6},{11,7},{8,8},{1,9},{14... | collective-permute-start | bytes 786440 | tf_op jit(solution)/shard_map/ppermute | solution.py:240
  25.3 61.3 %copy-start.1 = (bf16[512,224]{0,1:T(8,128)(2,1)S(1)}, bf16[512,224]{0,1:T(8,128)(2,1)}, u32[]{:S(2)}) copy-start(bf16[512,224]{0,1:T(8,128)(2,1)} %param.9) | copy-start | bytes 688132
  25.3 22.4 %collective-permute-start.1 = (bf16[2,224,512]{2,1,0:T(8,128)(2,1)S(1)}, bf16[2,224,512]{2,1,0:T(8,128)(2,1)S(1)}, u32[]{:S(2)}, u32[]{:S(2)}) collective-permute-start(bf16[2,224,512]{2,1,0:T(8,128)(2,1)S(1)} %bitcast.21), channel_id=1, source_target_pairs={{0,2},{1,15},{2,4},{3,1},{4,6},{5,3},{6,8},{7,5},{8,10},{9,7},{10,... | collective-permute-start | bytes 1376264 | tf_op jit(solution)/shard_map/ppermute | solution.py:229
  35.8 29.9 %all-to-all-start.1 = ((bf16[32,72,128]{2,1,0:T(8,128)(2,1)}), bf16[32,72,128]{2,1,0:T(8,128)(2,1)S(1)}, u32[]{:S(2)}, u32[]{:S(2)}) async-start(bf16[32,72,128]{2,1,0:T(8,128)(2,1)} %bitcast.7), calls=%async_computation.1 | async-start | bytes 1179648 | tf_op jit(solution)/shard_map/all_to_all | solution.py:187
  47.7 10.3 %collective-permute-start.2 = (bf16[2,224,512]{2,1,0:T(8,128)(2,1)S(1)}, bf16[2,224,512]{2,1,0:T(8,128)(2,1)S(1)}, u32[]{:S(2)}, u32[]{:S(2)}) collective-permute-start(bf16[2,224,512]{2,1,0:T(8,128)(2,1)S(1)} %collective-permute-done.1.refs_1_), channel_id=1, source_target_pairs={{0,2},{1,15},{2,4},{3,1},{4,6},{5,3},{6,8},{7,5},{8,10},{9,7},{10,... | collective-permute-start | bytes 1376264 | tf_op jit(solution)/shard_map/ppermute | solution.py:229
  58.0 15.7 %collective-permute-start.3 = (bf16[2,224,512]{2,1,0:T(8,128)(2,1)S(1)}, bf16[2,224,512]{2,1,0:T(8,128)(2,1)S(1)}, u32[]{:S(2)}, u32[]{:S(2)}) collective-permute-start(bf16[2,224,512]{2,1,0:T(8,128)(2,1)S(1)} %collective-permute-done.2.refs_2_), channel_id=1, source_target_pairs={{0,2},{1,15},{2,4},{3,1},{4,6},{5,3},{6,8},{7,5},{8,10},{9,7},{10,... | collective-permute-start | bytes 1376264 | tf_op jit(solution)/shard_map/ppermute | solution.py:229
  66.8 16.1 %all-to-all-start.2 = ((bf16[32,16,128]{2,1,0:T(8,128)(2,1)}), bf16[32,16,128]{2,1,0:T(8,128)(2,1)S(1)}, u32[]{:S(2)}, u32[]{:S(2)}) async-start(bf16[32,16,128]{2,1,0:T(8,128)(2,1)} %shard_map.57), calls=%async_computation.2 | async-start | bytes 262144 | tf_op jit(solution)/shard_map/all_to_all | solution.py:187
  73.8 12.8 %collective-permute-start.4 = (bf16[224,512]{1,0:T(8,128)(2,1)S(1)}, bf16[224,512]{1,0:T(8,128)(2,1)S(1)}, u32[]{:S(2)}, u32[]{:S(2)}) collective-permute-start(bf16[224,512]{1,0:T(8,128)(2,1)S(1)} %dynamic-slice_bitcast_fusion), channel_id=1, source_target_pairs={{0,2},{1,15},{2,4},{3,1},{4,6},{5,3},{6,8},{7,5},{8,10},{9,7},{10,... | collective-permute-start | bytes 688136 | tf_op jit(solution)/shard_map/ppermute | solution.py:231

commit v6 on v5

--- a/solution.py
+++ b/solution.py
@@ -66,9 +66,16 @@
     step = lax.rem(row, ahead)
     lane = lax.broadcasted_iota(jnp.int32, (all_rows, LANES), 1)
     start, core = scalars_ref[seqs + 1], scalars_ref[seqs + 2]
-    copies = [pltpu.make_async_copy(cache_ref.at[b], keys_ref.at[b], sems.at[b]) for b in range(seqs)]
-    for copy in copies:
-        copy.start()
+    copies = []
+    for b in range(seqs):
+        pieces = PARTS if b == 0 else 1
+        size = width // pieces
+        for k in range(pieces):
+            at = pl.ds(k * size, size)
+            copies.append(
+                pltpu.make_async_copy(cache_ref.at[b, at], keys_ref.at[b, at], sems.at[len(copies)])
+            )
+            copies[-1].start()
     part = ctx_dev // PARTS
     rest = q_ref[:, seqs * whole].reshape(all_rows, LANES)
 
@@ -82,11 +89,12 @@
         return jnp.where(position < limit, scores, NEG)
 
     extra = jnp.zeros((all_rows, LANES), jnp.float32)
-    copies[0].wait()
+    for copy in copies[:PARTS]:
+        copy.wait()
     scores = [masked_scores(0, k) for k in range(PARTS)]
     for b in range(seqs):
         if b + 1 < seqs:
-            copies[b + 1].wait()
+            copies[PARTS + b].wait()
         top = jnp.max(scores[0], axis=1, keepdims=True)
         for one in scores[1:]:
             top = jnp.maximum(top, jnp.max(one, axis=1, keepdims=True))
@@ -250,7 +258,7 @@
         up[:, :16],
         scratch=[
             pltpu.VMEM((seqs, width, ctx_dev), bf16),
-            pltpu.SemaphoreType.DMA((seqs,)),
+            pltpu.SemaphoreType.DMA((PARTS + seqs - 1,)),
         ],
         limit=52,
     )

time: 90.8 us -> 90.7 us (level)
  transfers between devices with their start and end apart: 8 -> 8, of which waited for: 3 -> 3; matrix products, arithmetic and copies ran while one was open for 1% -> 1% of each run, Pallas kernels for 9% -> 8%
where the time goes in v6:
time: 90.7 us; the launch traced here: 90.2 us
  starting transfers between devices  56.4 us (62%)
  waiting for transfers between devices  13.7 us (15%)
  Pallas kernels  9.77 us (11%)
  blocking collectives  7.87 us (9%)
  local copies, waits for them, and re-layouts  1.45 us (2%)
    all_to_all x3, starting transfers between devices, exchange(): return lax.all_to_all(flat, 'seq', 0, 0, tiled=True).reshape(blocks.shape)  29.4 us
    ppermute x3, starting transfers between devices, per_device(): block = lax.ppermute(block, batch, ring)  13.4 us
    ppermute x1, starting transfers between devices, per_device(): up = lax.ppermute(mine, ('seq', 'z', 'core'), pairs)  10.6 us
    pallas_call x4, Pallas kernels, call(): pl.pallas_call(kernel, out_shape=jax.ShapeDtypeStruct(shape, dtype), in_s...  9.77 us
    all_to_all x3, waiting for transfers between devices, exchange(): return lax.all_to_all(flat, 'seq', 0, 0, tiled=True).reshape(blocks.shape)  8.32 us
    ppermute x3, waiting for transfers between devices, per_device(): block = lax.ppermute(block, batch, ring)  5.41 us
    all_gather x1, blocking collectives, per_device(): lax.all_gather(values, 'core')  3.67 us
    ppermute x1, starting transfers between devices, per_device(): lax.ppermute(lax.dynamic_index_in_dim(block, core, 0, False), batch, ring)  2.98 us
  transfers between devices with their start and end apart: 8, of which 3 were waited for; matrix products, arithmetic and copies ran while one was open for 1% of the time, Pallas kernels for 8%

profile of v6, /device:TPU:1, one launch (start us, length us, event | category | flops | bytes accessed | tf_op | source)
XLA Modules:
  0.0 90.2 jit_solution(9049444843629416309)
XLA Ops:
  0.0 0.0 copy-start
  0.0 0.0 copy-start.2
  0.0 0.8 copy-done.2
  0.8 0.9 %shard_map.55 = bf16[32,9,8,128]{3,2,1,0:T(8,128)(2,1)} custom-call(bf16[2,4,2,576]{3,2,1,0:T(2,128)(2,1)S(1)} %copy-done.2), custom_call_target="tpu_custom_call" | custom-call | tf_op jit(solution)/shard_map/pallas_call | solution.py:199
  1.7 10.5 %all-to-all-start = ((bf16[32,72,128]{2,1,0:T(8,128)(2,1)}), bf16[32,72,128]{2,1,0:T(8,128)(2,1)S(1)}, u32[]{:S(2)}, u32[]{:S(2)}) async-start(bf16[32,72,128]{2,1,0:T(8,128)(2,1)} %bitcast.4), calls=%async_computation | async-start | bytes 1179648 | tf_op jit(solution)/shard_map/all_to_all | solution.py:195
  12.2 0.0 copy-done
  12.3 10.6 %collective-permute-start = (bf16[2,512,128]{2,1,0:T(8,128)(2,1)S(1)}, bf16[2,512,128]{2,1,0:T(8,128)(2,1)S(1)}, u32[]{:S(2)}, u32[]{:S(2)}) collective-permute-start(bf16[2,512,128]{2,1,0:T(8,128)(2,1)S(1)} %constant_dynamic-slice_fusion), channel_id=1, source_target_pairs={{0,0},{9,1},{6,2},{15,3},{12,4},{5,5},{2,6},{11,7},{8,8},{1,9},{14... | collective-permute-start | bytes 786440 | tf_op jit(solution)/shard_map/ppermute | solution.py:248
  22.9 2.3 %all-gather.1 = bf16[448,512]{1,0:T(8,128)(2,1)S(1)} all-gather(bf16[224,512]{1,0:T(8,128)(2,1)} %bitcast.18), channel_id=3, replica_groups=mesh['seq'=32,'z'=8,'core'=2] {'core'}, dimensions={0}, use_global_device_ids=true | all-gather | bytes 688128 | tf_op jit(solution)/shard_map/all_gather | solution.py:234
  25.3 0.0 copy-start.1
  25.3 3.2 %collective-permute-start.1 = (bf16[2,224,512]{2,1,0:T(8,128)(2,1)S(1)}, bf16[2,224,512]{2,1,0:T(8,128)(2,1)S(1)}, u32[]{:S(2)}, u32[]{:S(2)}) collective-permute-start(bf16[2,224,512]{2,1,0:T(8,128)(2,1)S(1)} %bitcast.21), channel_id=1, source_target_pairs={{0,2},{1,15},{2,4},{3,1},{4,6},{5,3},{6,8},{7,5},{8,10},{9,7},{10,... | collective-permute-start | bytes 1376264 | tf_op jit(solution)/shard_map/ppermute | solution.py:237
  28.5 0.7 pad_add_fusion.1.scalars_ref
  29.2 0.0 collective-permute-done.up_ref
  29.2 0.0 all-to-all-done
  29.2 6.5 %shard_map.56 = bf16[32,9,8,128]{3,2,1,0:T(8,128)(2,1)} custom-call(s32[5]{0:T(128)S(1)} %pad_add_fusion.1.scalars_ref, bf16[32,9,8,128]{3,2,1,0:T(8,128)(2,1)S(1)} %bitcast.15, bf16[2,576,2048]{2,1,0:T(8,128)(2,1)} %bitcast.20, bf16[2,16,128]{2,1,0:T(8,128)(2,1)S(1)} %slice.4.up_ref), custom_call_target="tpu_custom_call" | custom-call | tf_op jit(solution)/shard_map/pallas_call | solution.py:199
  35.7 11.9 %all-to-all-start.1 = ((bf16[32,72,128]{2,1,0:T(8,128)(2,1)}), bf16[32,72,128]{2,1,0:T(8,128)(2,1)S(1)}, u32[]{:S(2)}, u32[]{:S(2)}) async-start(bf16[32,72,128]{2,1,0:T(8,128)(2,1)} %bitcast.7), calls=%async_computation.1 | async-start | bytes 1179648 | tf_op jit(solution)/shard_map/all_to_all | solution.py:195
  47.7 0.0 collective-permute-done.1.refs_1_
  47.7 4.9 %collective-permute-start.2 = (bf16[2,224,512]{2,1,0:T(8,128)(2,1)S(1)}, bf16[2,224,512]{2,1,0:T(8,128)(2,1)S(1)}, u32[]{:S(2)}, u32[]{:S(2)}) collective-permute-start(bf16[2,224,512]{2,1,0:T(8,128)(2,1)S(1)} %collective-permute-done.1.refs_1_), channel_id=1, source_target_pairs={{0,2},{1,15},{2,4},{3,1},{4,6},{5,3},{6,8},{7,5},{8,10},{9,7},{10,... | collective-permute-start | bytes 1376264 | tf_op jit(solution)/shard_map/ppermute | solution.py:237
  52.6 5.4 %collective-permute-done.2.refs_2_ = bf16[2,224,512]{2,1,0:T(8,128)(2,1)S(1)} collective-permute-done((bf16[2,224,512]{2,1,0:T(8,128)(2,1)S(1)}, bf16[2,224,512]{2,1,0:T(8,128)(2,1)S(1)}, u32[]{:S(2)}, u32[]{:S(2)}) %collective-permute-start.2) | collective-permute-done | bytes 458784 | tf_op jit(solution)/shard_map/ppermute | solution.py:237
  58.0 5.3 %collective-permute-start.3 = (bf16[2,224,512]{2,1,0:T(8,128)(2,1)S(1)}, bf16[2,224,512]{2,1,0:T(8,128)(2,1)S(1)}, u32[]{:S(2)}, u32[]{:S(2)}) collective-permute-start(bf16[2,224,512]{2,1,0:T(8,128)(2,1)S(1)} %collective-permute-done.2.refs_2_), channel_id=1, source_target_pairs={{0,2},{1,15},{2,4},{3,1},{4,6},{5,3},{6,8},{7,5},{8,10},{9,7},{10,... | collective-permute-start | bytes 1376264 | tf_op jit(solution)/shard_map/ppermute | solution.py:237
  63.3 2.3 %all-to-all-done.1 = bf16[32,72,128]{2,1,0:T(8,128)(2,1)S(1)} async-done(((bf16[32,72,128]{2,1,0:T(8,128)(2,1)}), bf16[32,72,128]{2,1,0:T(8,128)(2,1)S(1)}, u32[]{:S(2)}, u32[]{:S(2)}) %all-to-all-start.1) | async-done | bytes 589856 | tf_op jit(solution)/shard_map/all_to_all | solution.py:195
  65.6 1.2 %shard_map.57 = bf16[32,16,128]{2,1,0:T(8,128)(2,1)} custom-call(bf16[32,9,8,128]{3,2,1,0:T(8,128)(2,1)S(1)} %bitcast.16, bf16[2,512,128]{2,1,0:T(8,128)(2,1)S(1)} %collective-permute-done.up_ref), custom_call_target="tpu_custom_call" | custom-call | tf_op jit(solution)/shard_map/pallas_call | solution.py:199
  66.7 7.0 %all-to-all-start.2 = ((bf16[32,16,128]{2,1,0:T(8,128)(2,1)}), bf16[32,16,128]{2,1,0:T(8,128)(2,1)S(1)}, u32[]{:S(2)}, u32[]{:S(2)}) async-start(bf16[32,16,128]{2,1,0:T(8,128)(2,1)} %shard_map.57), calls=%async_computation.2 | async-start | bytes 262144 | tf_op jit(solution)/shard_map/all_to_all | solution.py:195
  73.7 0.0 collective-permute-done.3.refs_3_
  73.8 3.0 %collective-permute-start.4 = (bf16[224,512]{1,0:T(8,128)(2,1)S(1)}, bf16[224,512]{1,0:T(8,128)(2,1)S(1)}, u32[]{:S(2)}, u32[]{:S(2)}) collective-permute-start(bf16[224,512]{1,0:T(8,128)(2,1)S(1)} %dynamic-slice_bitcast_fusion), channel_id=1, source_target_pairs={{0,2},{1,15},{2,4},{3,1},{4,6},{5,3},{6,8},{7,5},{8,10},{9,7},{10,... | collective-permute-start | bytes 688136 | tf_op jit(solution)/shard_map/ppermute | solution.py:239
  76.7 0.1 pad_add_fusion.place_ref
  76.8 6.0 %all-to-all-done.2 = bf16[32,16,128]{2,1,0:T(8,128)(2,1)S(1)} async-done(((bf16[32,16,128]{2,1,0:T(8,128)(2,1)}), bf16[32,16,128]{2,1,0:T(8,128)(2,1)S(1)}, u32[]{:S(2)}, u32[]{:S(2)}) %all-to-all-start.2) | async-done | bytes 131104 | tf_op jit(solution)/shard_map/all_to_all | solution.py:195
  82.9 3.7 %all-gather = bf16[64,16,128]{2,1,0:T(8,128)(2,1)S(1)} all-gather(bf16[32,16,128]{2,1,0:T(8,128)(2,1)S(1)} %all-to-all-done.2), channel_id=2, replica_groups=mesh['seq'=32,'z'=8,'core'=2] {'core'}, dimensions={0}, use_global_device_ids=true | all-gather | bytes 393216 | tf_op jit(solution)/shard_map/all_gather | solution.py:281
  86.5 0.0 collective-permute-done.4.refs_4_
  86.5 0.0 copy-done.1
  86.5 1.2 %shard_map.58 = f32[2,8,224]{2,1,0:T(8,128)S(1)} custom-call(s32[2]{0:T(128)S(1)} %pad_add_fusion.place_ref, bf16[2,32,16,128]{3,2,1,0:T(8,128)(2,1)S(1)} %bitcast.17, bf16[224,512]{1,0:T(8,128)(2,1)S(1)} %bitcast.19, bf16[2,224,512]{2,1,0:T(8,128)(2,1)S(1)} %collective-permute-done.1.refs_1_, bf16[2,224,512]{2,1,0:T(8,128)(2,1)S(1)} %collective-permute-done.2.refs_2_, ...), custom_call_target="tpu_custom_call" | custom-call | tf_op jit(solution)/shard_map/pallas_call | solution.py:199
  87.7 1.9 %all-gather.2 = f32[4,8,224]{2,1,0:T(8,128)S(1)} all-gather(f32[2,8,224]{2,1,0:T(8,128)S(1)} %shard_map.58), channel_id=4, replica_groups=mesh['seq'=32,'z'=8,'core'=2] {'core'}, dimensions={0}, use_global_device_ids=true | all-gather | bytes 43008 | tf_op jit(solution)/shard_map/all_gather | solution.py:284
  89.6 0.6 convert_element_type.7
  (4 shorter events, 0.1 us)
Async XLA Ops:
  0.0 12.2 %copy-start = (bf16[4,512,128]{2,1,0:T(8,128)(2,1)S(1)}, bf16[4,512,128]{2,1,0:T(8,128)(2,1)}, u32[]{:S(2)}) copy-start(bf16[4,512,128]{2,1,0:T(8,128)(2,1)} %param.8) | copy-start | bytes 1572868
  0.0 0.8 copy-start.2
  1.7 27.5 %all-to-all-start = ((bf16[32,72,128]{2,1,0:T(8,128)(2,1)}), bf16[32,72,128]{2,1,0:T(8,128)(2,1)S(1)}, u32[]{:S(2)}, u32[]{:S(2)}) async-start(bf16[32,72,128]{2,1,0:T(8,128)(2,1)} %bitcast.4), calls=%async_computation | async-start | bytes 1179648 | tf_op jit(solution)/shard_map/all_to_all | solution.py:195
  12.3 16.9 %collective-permute-start = (bf16[2,512,128]{2,1,0:T(8,128)(2,1)S(1)}, bf16[2,512,128]{2,1,0:T(8,128)(2,1)S(1)}, u32[]{:S(2)}, u32[]{:S(2)}) collective-permute-start(bf16[2,512,128]{2,1,0:T(8,128)(2,1)S(1)} %constant_dynamic-slice_fusion), channel_id=1, source_target_pairs={{0,0},{9,1},{6,2},{15,3},{12,4},{5,5},{2,6},{11,7},{8,8},{1,9},{14... | collective-permute-start | bytes 786440 | tf_op jit(solution)/shard_map/ppermute | solution.py:248
  25.3 61.3 %copy-start.1 = (bf16[512,224]{0,1:T(8,128)(2,1)S(1)}, bf16[512,224]{0,1:T(8,128)(2,1)}, u32[]{:S(2)}) copy-start(bf16[512,224]{0,1:T(8,128)(2,1)} %param.9) | copy-start | bytes 688132
  25.3 22.4 %collective-permute-start.1 = (bf16[2,224,512]{2,1,0:T(8,128)(2,1)S(1)}, bf16[2,224,512]{2,1,0:T(8,128)(2,1)S(1)}, u32[]{:S(2)}, u32[]{:S(2)}) collective-permute-start(bf16[2,224,512]{2,1,0:T(8,128)(2,1)S(1)} %bitcast.21), channel_id=1, source_target_pairs={{0,2},{1,15},{2,4},{3,1},{4,6},{5,3},{6,8},{7,5},{8,10},{9,7},{10,... | collective-permute-start | bytes 1376264 | tf_op jit(solution)/shard_map/ppermute | solution.py:237
  35.7 29.9 %all-to-all-start.1 = ((bf16[32,72,128]{2,1,0:T(8,128)(2,1)}), bf16[32,72,128]{2,1,0:T(8,128)(2,1)S(1)}, u32[]{:S(2)}, u32[]{:S(2)}) async-start(bf16[32,72,128]{2,1,0:T(8,128)(2,1)} %bitcast.7), calls=%async_computation.1 | async-start | bytes 1179648 | tf_op jit(solution)/shard_map/all_to_all | solution.py:195
  47.7 10.3 %collective-permute-start.2 = (bf16[2,224,512]{2,1,0:T(8,128)(2,1)S(1)}, bf16[2,224,512]{2,1,0:T(8,128)(2,1)S(1)}, u32[]{:S(2)}, u32[]{:S(2)}) collective-permute-start(bf16[2,224,512]{2,1,0:T(8,128)(2,1)S(1)} %collective-permute-done.1.refs_1_), channel_id=1, source_target_pairs={{0,2},{1,15},{2,4},{3,1},{4,6},{5,3},{6,8},{7,5},{8,10},{9,7},{10,... | collective-permute-start | bytes 1376264 | tf_op jit(solution)/shard_map/ppermute | solution.py:237
  58.0 15.7 %collective-permute-start.3 = (bf16[2,224,512]{2,1,0:T(8,128)(2,1)S(1)}, bf16[2,224,512]{2,1,0:T(8,128)(2,1)S(1)}, u32[]{:S(2)}, u32[]{:S(2)}) collective-permute-start(bf16[2,224,512]{2,1,0:T(8,128)(2,1)S(1)} %collective-permute-done.2.refs_2_), channel_id=1, source_target_pairs={{0,2},{1,15},{2,4},{3,1},{4,6},{5,3},{6,8},{7,5},{8,10},{9,7},{10,... | collective-permute-start | bytes 1376264 | tf_op jit(solution)/shard_map/ppermute | solution.py:237
  66.7 16.1 %all-to-all-start.2 = ((bf16[32,16,128]{2,1,0:T(8,128)(2,1)}), bf16[32,16,128]{2,1,0:T(8,128)(2,1)S(1)}, u32[]{:S(2)}, u32[]{:S(2)}) async-start(bf16[32,16,128]{2,1,0:T(8,128)(2,1)} %shard_map.57), calls=%async_computation.2 | async-start | bytes 262144 | tf_op jit(solution)/shard_map/all_to_all | solution.py:195
  73.8 12.8 %collective-permute-start.4 = (bf16[224,512]{1,0:T(8,128)(2,1)S(1)}, bf16[224,512]{1,0:T(8,128)(2,1)S(1)}, u32[]{:S(2)}, u32[]{:S(2)}) collective-permute-start(bf16[224,512]{1,0:T(8,128)(2,1)S(1)} %dynamic-slice_bitcast_fusion), channel_id=1, source_target_pairs={{0,2},{1,15},{2,4},{3,1},{4,6},{5,3},{6,8},{7,5},{8,10},{9,7},{10,... | collective-permute-start | bytes 688136 | tf_op jit(solution)/shard_map/ppermute | solution.py:239
